TPU v7x, 32 devices: a whole 2x2x4 slice. The times are simulated.
32 devices in a mesh: req: 4 (over z), head: 2 (over core), grp: 4 (over y, x).
Axes of the slice: x: 2, y: 2, z: 4, core: 2. Of those that a mesh axis runs over, the one named last changes fastest.
Arguments:
- residual: bfloat16 [128, 7168], P(('req', 'grp'), 'head'), may hold values from -12 to 12
- attn_part: bfloat16 [2, 128, 7168], P('head', ('req', 'grp')), may hold values from -6 to 6
- norm_gain: float32 [7168], P('head'), may hold values from 0.1 to 1.9
- routes: int32 [128, 8], P(('req', 'grp')), may hold values from 0 to 31, all different within a row; in each aligned block of 8 rows (0 to 7, 8 to 15, ...) at most 4 rows name the same one
- gates: float32 [128, 8], P(('req', 'grp')), may hold values from 0.1 to 0.6
- gate_weight: bfloat16 [32, 7168, 2048], P('req', None, ('head', 'grp')), may hold values from -0.0625 to 0.0625
- up_weight: bfloat16 [32, 7168, 2048], P('req', None, ('head', 'grp')), may hold values from -0.0625 to 0.0625
- down_weight: bfloat16 [32, 2048, 7168], P('req', None, ('head', 'grp')), may hold values from -0.125 to 0.125
Outputs:
- mixed: bfloat16 [128, 7168], P(('req', 'grp'), 'head')
Inputs may be any that keep to these rules, and one draw needn't show every extreme that they name: `routes`: each row names 8 different experts. In each aligned block of 8 rows (the rows of one index pair of req and grp) no expert is named more than 4 times, a bound that some block reaches.
All inputs are finite; a program needn't handle non-finite values.
Results may differ from a plain program's by a relative error of at most 0.012.
Values may be sent and summed in bfloat16 or wider, within the bound.
No kernel may reach another device: no remote copies, remote signals or barrier semaphores. Data moves between devices by JAX's collectives and lax.ppermute only.
A program may use at most 192 MiB of HBM per device.

v0:
```python
import jax
import jax.numpy as jnp
from jax import lax
from jax.sharding import PartitionSpec as P

D = 7168
CAP = 4


EPSILON = 1e-06


def slot_places(routes, experts):
    count_rows, count_top = routes.shape
    flat_routes = routes.reshape(count_rows * count_top)
    onehot = (flat_routes[:, None] == jnp.arange(experts, dtype=jnp.int32)[None, :]).astype(
        jnp.int32
    )
    earlier = jnp.cumsum(onehot, axis=0) - onehot
    slot_index = jnp.sum(earlier * onehot, axis=1).reshape(count_rows, count_top)
    return routes * CAP + slot_index


def select_table(places, experts):
    return places[:, :, None] == jnp.arange(experts * CAP, dtype=jnp.int32)[None, None, :]


def expert_hidden(arrived, gate_weight, up_weight):
    groups, sources, columns, features = arrived.shape
    local_experts = gate_weight.shape[0]
    shaped = arrived.reshape(groups, sources, local_experts, columns // local_experts, features)
    gate_act = jnp.einsum(
        "gresd,edf->gresf", shaped, gate_weight, preferred_element_type=jnp.float32
    )
    up_act = jnp.einsum("gresd,edf->gresf", shaped, up_weight, preferred_element_type=jnp.float32)
    return (jax.nn.silu(gate_act) * up_act).astype(jnp.bfloat16)


def on_device(residual, attn_part, norm_gain, routes, gates, gate_weight, up_weight, down_weight):
    req_count = lax.axis_size("req")
    experts = gate_weight.shape[0] * req_count
    summed = lax.psum_scatter(
        attn_part[0].astype(jnp.float32).astype(jnp.bfloat16),
        "head",
        scatter_dimension=1,
        tiled=True,
    ).astype(jnp.float32)
    hidden_state = residual.astype(jnp.float32) + summed
    squares = lax.psum(jnp.sum(hidden_state * hidden_state, axis=1), "head")
    row_scale = lax.rsqrt(squares / D + EPSILON)
    normed = (hidden_state * row_scale[:, None] * norm_gain[None, :]).astype(jnp.bfloat16)
    selected = select_table(slot_places(routes, experts), experts)
    weighting = jnp.sum(jnp.where(selected, gates[:, :, None], 0.0), axis=1)
    packing = jnp.any(selected, axis=1).astype(jnp.bfloat16)
    packed = jnp.einsum("tj,td->jd", packing, normed, preferred_element_type=jnp.float32).astype(
        jnp.bfloat16
    )
    packed = packed.reshape(req_count, -1, normed.shape[1])
    arrived = lax.all_to_all(packed, "req", split_axis=0, concat_axis=0, tiled=True)
    whole_rows = lax.all_gather(arrived, "head", axis=2, tiled=True)
    hidden_units = expert_hidden(
        lax.all_gather(whole_rows[None], "grp", axis=0, tiled=True), gate_weight, up_weight
    )
    projected = jnp.einsum(
        "gresf,efd->gresd",
        lax.all_gather(hidden_units, ("head", "grp"), axis=4, tiled=True),
        down_weight,
        preferred_element_type=jnp.float32,
    )
    outgoing = projected.astype(jnp.bfloat16)
    regrouped = lax.all_to_all(outgoing, "grp", split_axis=0, concat_axis=4, tiled=True)
    regrouped = regrouped.reshape(req_count, -1, regrouped.shape[4])
    returned = lax.all_to_all(regrouped, "req", split_axis=0, concat_axis=0, tiled=True)
    back_rows = returned.reshape(-1, returned.shape[-1]).astype(jnp.float32)
    routed = jnp.dot(weighting, back_rows, precision=lax.Precision.HIGHEST)
    return (hidden_state + routed).astype(jnp.bfloat16)


def solution(mesh):
    placed = (
        P(("req", "grp"), "head"),
        P("head", ("req", "grp"), None),
        P("head"),
        P(("req", "grp"), None),
        P(("req", "grp"), None),
        P("req", None, ("head", "grp")),
        P("req", None, ("head", "grp")),
        P("req", None, ("head", "grp")),
    )
    return jax.shard_map(
        on_device, mesh=mesh, in_specs=placed, out_specs=P(("req", "grp"), "head"), check_vma=False
    )
```

profile of v0, /device:TPU:0, one launch (start us, length us, event | category | flops | bytes accessed | tf_op | source)
XLA Modules:
  0.0 284.0 jit_solution(13800154999178209875)
XLA Ops:
  6.5 0.0 reduce-scatter.2.cloned.1.call-start
  6.5 0.7 reduce-scatter.2.cloned.1.call-update
  7.3 0.0 all-gather.5.cloned.1.call-start
  7.3 0.8 eq.28
  8.1 0.1 fusion.38
  8.1 0.1 reduce_window_sum.11
  8.2 0.2 select_reduce_fusion.1
  8.4 0.1 reshape.21
  8.5 0.7 multiply_add_fusion
  9.2 10.6 %reduce-scatter.2.cloned.1.call-done = bf16[8,3584]{1,0:T(8,128)(2,1)} async-done(((bf16[8,7168]{1,0:T(8,128)(2,1)}), bf16[8,3584]{1,0:T(8,128)(2,1)}) %reduce-scatter.2.cloned.1.call-update) | async-done | bytes 57360 | tf_op jit(solution)/shard_map/reduce_scatter | solution.py:42
  19.8 1.0 multiply_reduce_fusion
  20.8 0.1 fusion.37
  20.9 2.5 psum.7
  23.4 1.3 convolution_convert_fusion
  24.7 28.1 %all_to_all.25 = bf16[4,32,3584]{2,1,0:T(8,128)(2,1)} all-to-all(bf16[4,32,3584]{2,1,0:T(8,128)(2,1)S(1)} %bitcast.47), channel_id=1, replica_groups=mesh['req'=4,'head'=2,'grp'=4] {'req'}, dimensions={0} | all-to-all | bytes 1835008 | tf_op jit(solution)/shard_map/all_to_all | solution.py:59
  52.8 0.0 all-gather.5.cloned.1.call-update
  52.8 0.0 all-gather.9.cloned.1.call-start
  52.9 9.4 %all-gather.5.cloned.1.call-done = bf16[4,32,7168]{2,1,0:T(8,128)(2,1)} async-done(((bf16[4,32,3584]{2,1,0:T(8,128)(2,1)}), bf16[4,32,7168]{2,1,0:T(8,128)(2,1)}) %all-gather.5.cloned.1.call-update) | async-done | bytes 1835024 | tf_op jit(solution)/shard_map/all_gather | solution.py:60
  62.2 0.0 all-gather.9.cloned.1.call-update
  62.3 0.0 all-gather.7.cloned.1.call-start
  62.3 81.9 %all-gather.9.cloned.1.call-done = bf16[16,32,7168]{2,1,0:T(8,128)(2,1)} async-done(((bf16[4,32,7168]{2,1,0:T(8,128)(2,1)}), bf16[16,32,7168]{2,1,0:T(8,128)(2,1)}) %all-gather.9.cloned.1.call-update) | async-done | bytes 7340048 | tf_op jit(solution)/shard_map/all_gather | solution.py:62
  144.2 12.6 %reshape.23 = bf16[4,4,8,4,7168]{4,3,2,1,0:T(4,128)(2,1)} reshape(bf16[16,32,7168]{2,1,0:T(8,128)(2,1)} %all-gather.9.cloned.1.call-done) | data formatting | bytes 14680064 | tf_op jit(solution)/shard_map/reshape | solution.py:31
  156.8 14.8 %fusion.15 = f32[4,4,8,4,256]{4,3,1,0,2:T(4,128)S(1)} fusion(bf16[8,7168,256]{2,1,0:T(8,128)(2,1)} %param.13, bf16[4,4,8,4,7168]{4,3,2,1,0:T(4,128)(2,1)} %reshape.23), kind=kOutput, calls=%fused_computation.13 | convolution fusion | flops 1879048192 | bytes 37224448 | tf_op jit(solution)/shard_map/gresd,edf->gresf/dot_general | solution.py:32
  171.7 15.8 %fusion.30 = bf16[4,4,8,4,256]{4,3,1,0,2:T(4,128)(2,1)} fusion(bf16[8,7168,256]{2,1,0:T(8,128)(2,1)} %param.14, bf16[4,4,8,4,7168]{4,3,2,1,0:T(4,128)(2,1)} %reshape.23, f32[4,4,8,4,256]{4,3,1,0,2:T(4,128)S(1)} %fusion.15), kind=kOutput, calls=%fused_computation.16 | convolution fusion | flops 1879834624 | bytes 37486592 | tf_op jit(solution)/shard_map/gresd,edf->gresf/dot_general | solution.py:35
  187.4 0.0 all-gather.7.cloned.1.call-update
  187.5 28.4 %all-gather.7.cloned.1.call-done = bf16[4,4,8,4,2048]{4,3,1,0,2:T(4,128)(2,1)} async-done(((bf16[4,4,8,4,256]{4,3,1,0,2:T(4,128)(2,1)}), bf16[4,4,8,4,2048]{4,3,1,0,2:T(4,128)(2,1)}) %all-gather.7.cloned.1.call-update) | async-done | bytes 2097168 | tf_op jit(solution)/shard_map/all_gather | solution.py:66
  215.8 15.7 %fusion.12 = bf16[4,4,8,4,896]{4,3,1,0,2:T(4,128)(2,1)S(1)} fusion(bf16[4,4,8,4,2048]{4,3,1,0,2:T(4,128)(2,1)} %all-gather.7.cloned.1.call-done, bf16[8,2048,896]{2,1,0:T(8,128)(2,1)} %param.15), kind=kOutput, calls=%fused_computation.12 | convolution fusion | flops 1879506944 | bytes 32374784 | tf_op jit(solution)/shard_map/gresf,efd->gresd/dot_general | solution.py:64
  231.6 0.0 copy-start.2
  231.6 0.0 copy-start
  231.6 0.0 copy-start.1
  231.6 0.3 copy.17
  231.9 15.9 %all_to_all.26 = bf16[4,4,8,4,896]{4,3,1,2,0:T(4,128)(2,1)S(1)} all-to-all(bf16[4,4,8,4,896]{4,3,1,2,0:T(4,128)(2,1)S(1)} %copy.17), channel_id=1, replica_groups=mesh['req'=4,'head'=2,'grp'=4] {'grp'}, dimensions={0} | all-to-all | bytes 1835008 | tf_op jit(solution)/shard_map/all_to_all | solution.py:71
  247.8 0.7 copy.18
  248.5 1.3 reshape.24
  249.8 4.6 %all-to-all-start.2 = ((bf16[4,32,3584]{2,1,0:T(8,128)(2,1)}), bf16[4,32,3584]{2,1,0:T(8,128)(2,1)S(1)}, u32[]{:S(2)}, u32[]{:S(2)}) async-start(bf16[4,32,3584]{2,1,0:T(8,128)(2,1)} %reshape.24), calls=%async_computation.3 | async-start | bytes 1835008 | tf_op jit(solution)/shard_map/all_to_all | solution.py:73
  254.4 0.0 copy-done.2
  254.4 0.1 select_reduce_fusion
  254.5 21.9 %all-to-all-done.2 = bf16[4,32,3584]{2,1,0:T(8,128)(2,1)S(1)} async-done(((bf16[4,32,3584]{2,1,0:T(8,128)(2,1)}), bf16[4,32,3584]{2,1,0:T(8,128)(2,1)S(1)}, u32[]{:S(2)}, u32[]{:S(2)}) %all-to-all-start.2) | async-done | bytes 917536 | tf_op jit(solution)/shard_map/all_to_all | solution.py:73
  276.4 0.0 copy-done
  276.4 0.0 copy-done.1
  276.4 1.1 fusion.8
  (1 shorter events, 0.0 us)
Async XLA Ops:
  6.5 13.3 %reduce-scatter.2.cloned.1.call-start = ((), (), s32[]{:S(2)}) async-start(), calls=%async_computation.4 | async-start | bytes 172032 | tf_op jit(solution)/shard_map/reduce_scatter | solution.py:42
  7.3 55.0 %all-gather.5.cloned.1.call-start = ((), (), s32[]{:S(2)}) async-start(), calls=%async_computation.5 | async-start | bytes 2752512 | tf_op jit(solution)/shard_map/all_gather | solution.py:60
  52.8 91.3 %all-gather.9.cloned.1.call-start = ((), (), s32[]{:S(2)}) async-start(), calls=%async_computation.7 | async-start | bytes 9175040 | tf_op jit(solution)/shard_map/all_gather | solution.py:62
  62.3 153.5 %all-gather.7.cloned.1.call-start = ((), (), s32[]{:S(2)}) async-start(), calls=%async_computation.6 | async-start | bytes 2359296 | tf_op jit(solution)/shard_map/all_gather | solution.py:66
  231.6 22.8 %copy-start.2 = (f32[8,8]{1,0:T(8,128)S(1)}, f32[8,8]{1,0:T(8,128)}, u32[]{:S(2)}) copy-start(f32[8,8]{1,0:T(8,128)} %param.12) | copy-start | bytes 772
  231.6 44.8 %copy-start = (bf16[8,3584]{1,0:T(8,128)(2,1)S(1)}, bf16[8,3584]{1,0:T(8,128)(2,1)}, u32[]{:S(2)}) copy-start(bf16[8,3584]{1,0:T(8,128)(2,1)} %param.8) | copy-start | bytes 172036
  231.6 44.8 %copy-start.1 = (bf16[8,3584]{1,0:T(8,128)(2,1)S(1)}, bf16[8,3584]{1,0:T(8,128)(2,1)}, u32[]{:S(2)}) copy-start(bf16[8,3584]{1,0:T(8,128)(2,1)} %reduce-scatter.2.cloned.1.call-done) | copy-start | bytes 172036
  249.8 26.6 %all-to-all-start.2 = ((bf16[4,32,3584]{2,1,0:T(8,128)(2,1)}), bf16[4,32,3584]{2,1,0:T(8,128)(2,1)S(1)}, u32[]{:S(2)}, u32[]{:S(2)}) async-start(bf16[4,32,3584]{2,1,0:T(8,128)(2,1)} %reshape.24), calls=%async_computation.3 | async-start | bytes 1835008 | tf_op jit(solution)/shard_map/all_to_all | solution.py:73
Sparse Core Ops, SparseCore 0:
  9.6 10.1 reduce-scatter.1
  53.0 9.2 all-gather.4
  64.1 80.0 all-gather.8
  187.6 28.1 all-gather.6
where the time goes:
time: 285 us; the launch traced here: 284 us
  waiting for transfers between devices  153 us (54%)
  matrix products  48.7 us (17%)
  blocking collectives  46.5 us (16%)
  local copies, waits for them, and re-layouts  15.8 us (6%)
  between operations  13.2 us (5%)
  starting transfers between devices  4.72 us (2%)
    all_gather x1, waiting for transfers between devices, on_device(): lax.all_gather(whole_rows[None], 'grp', axis=0, tiled=True)  81.9 us
    all_gather x1, waiting for transfers between devices, on_device(): lax.all_gather(hidden_units, ('head', 'grp'), axis=4, tiled=True)  28.4 us
    all_to_all x1, blocking collectives, on_device(): lax.all_to_all(packed, 'req', split_axis=0, concat_axis=0, tiled=True)  28.1 us
    all_to_all x1, waiting for transfers between devices, on_device(): lax.all_to_all(regrouped, 'req', split_axis=0, concat_axis=0, tiled=True)  21.9 us
    all_to_all x1, blocking collectives, on_device(): lax.all_to_all(outgoing, 'grp', split_axis=0, concat_axis=4, tiled=True)  15.9 us
    dot_general x1, matrix products, expert_hidden(): jnp.einsum('gresd,edf->gresf', shaped, up_weight, preferred_element_type=...  15.8 us
    dot_general x1, matrix products, on_device(): jnp.einsum('gresf,efd->gresd', lax.all_gather(hidden_units, ('head', 'grp...  15.7 us
    dot_general x1, matrix products, expert_hidden(): jnp.einsum('gresd,edf->gresf', shaped, gate_weight, preferred_element_typ...  14.8 us
  transfers between devices with their start and end apart: 5, of which 5 were waited for; matrix products, arithmetic and copies ran while one was open for 1% of the time, Pallas kernels for 0%

commit v1 on v0

v1 whole, which is shorter than its diff:
```python
import jax
import jax.numpy as jnp
from jax import lax
from jax.experimental import pallas as pl
from jax.experimental.pallas import tpu as pltpu
from jax.sharding import PartitionSpec as P

CAP = 4
EPSILON = 1e-06
TAIL = 128
CUTS = 7
FLIGHT = 4
RING = 3
MIB = 1024 * 1024
VMEM = pl.BlockSpec(memory_space=pltpu.VMEM)
SMEM = pl.BlockSpec(memory_space=pltpu.SMEM)
ANY = pl.BlockSpec(memory_space=pl.ANY)
HBM = pl.BlockSpec(memory_space=pltpu.HBM)


def swap(array, axis, bits):
    return lax.ppermute(array, axis, [(i, i ^ bits) for i in range(lax.axis_size(axis))])


def gather_rows(array, axis, meanwhile):
    count = lax.axis_size(axis)
    if count > 4:
        return lax.all_gather(array, axis, axis=0, tiled=True), meanwhile
    pieces = [array] + [swap(array, axis, bits) for bits in range(1, count)]
    pieces, meanwhile = lax.optimization_barrier((pieces, meanwhile))

    def kernel(*refs):
        refs[-1][...] = jnp.concatenate([ref[...] for ref in refs[:-1]], axis=0)

    rows = pl.pallas_call(
        kernel,
        out_shape=jax.ShapeDtypeStruct((count * array.shape[0], array.shape[1]), array.dtype),
        in_specs=[VMEM] * count,
        out_specs=VMEM,
        compiler_params=pltpu.CompilerParams(vmem_limit_bytes=4 * MIB),
        name="collect",
    )(*pieces)
    return rows, meanwhile


def prepare_kernel(where_ref, *refs):
    sources, (base_ref, tail_ref, out_gain_ref), refs = refs[:5], refs[5:8], refs[8:]
    copies_to, wide_ref, sems = refs[:4], refs[4], refs[5]
    copies = [
        pltpu.make_async_copy(source, target, sems.at[index])
        for index, (source, target) in enumerate(zip(sources, (*copies_to, out_gain_ref)))
    ]
    for copy in copies:
        copy.start()
    for copy in copies:
        copy.wait()
    attn_ref, res_ref, routes_ref, gates_ref = copies_to
    half = res_ref.shape[1]
    top = routes_ref.shape[1]
    here = pl.ds(pl.multiple_of(where_ref[0] * half, 128), half)
    base_ref[...] = attn_ref[...].astype(jnp.float32)
    base_ref[:, here] += res_ref[...].astype(jnp.float32)
    gates = gates_ref[...]
    upper = gates.astype(jnp.bfloat16).astype(jnp.float32)
    middle = (gates - upper).astype(jnp.bfloat16).astype(jnp.float32)
    wide_ref[...] = jnp.zeros_like(wide_ref)
    for index, part in enumerate((routes_ref[...].astype(jnp.float32), upper, middle, gates - upper - middle)):
        wide_ref[:, index * top : (index + 1) * top] = part
    tail_ref[...] = wide_ref[...].astype(jnp.bfloat16)


def prepare(where, attn, residual, routes, gates, gain):
    rows = residual.shape[0]
    arrays = [attn, residual, routes, gates]
    return pl.pallas_call(
        prepare_kernel,
        out_shape=(
            jax.ShapeDtypeStruct(attn.shape, jnp.float32),
            jax.ShapeDtypeStruct((rows, TAIL), jnp.bfloat16),
            jax.ShapeDtypeStruct(gain.shape, jnp.float32),
        ),
        in_specs=[SMEM] + [HBM] * 5,
        out_specs=(VMEM, VMEM, VMEM),
        scratch_shapes=[pltpu.VMEM(array.shape, array.dtype) for array in arrays]
        + [pltpu.VMEM((rows, TAIL), jnp.float32), pltpu.SemaphoreType.DMA((5,))],
        compiler_params=pltpu.CompilerParams(vmem_limit_bytes=4 * MIB),
        name="prepare",
    )(where, *[in_hbm(array) for array in (*arrays, gain)])


def norm_kernel(where_ref, base_ref, attn_there_ref, res_there_ref, gain_ref, tail_ref, hidden_ref, packet_ref):
    half = res_there_ref.shape[1]
    here = pl.ds(pl.multiple_of(where_ref[0] * half, 128), half)
    there = pl.ds(pl.multiple_of((1 - where_ref[0]) * half, 128), half)
    hidden = base_ref[:, here] + attn_there_ref[:, here].astype(jnp.float32)
    other = base_ref[:, there] + attn_there_ref[:, there].astype(jnp.float32) + res_there_ref[...].astype(jnp.float32)
    squares = jnp.sum(hidden * hidden, axis=1, keepdims=True) + jnp.sum(other * other, axis=1, keepdims=True)
    row_scale = lax.rsqrt(squares / (2 * half) + EPSILON)
    hidden_ref[...] = hidden
    packet_ref[:, :half] = (hidden * row_scale * gain_ref[...]).astype(jnp.bfloat16)
    packet_ref[:, half:] = tail_ref[...]


def norm(where, base, attn_there, residual_there, gain, tail):
    rows, half = residual_there.shape
    return pl.pallas_call(
        norm_kernel,
        out_shape=(
            jax.ShapeDtypeStruct((rows, half), jnp.float32),
            jax.ShapeDtypeStruct((rows, half + TAIL), jnp.bfloat16),
        ),
        in_specs=[SMEM] + [VMEM] * 5,
        out_specs=(VMEM, VMEM),
        compiler_params=pltpu.CompilerParams(vmem_limit_bytes=4 * MIB),
        name="norm",
    )(where, base, attn_there, residual_there, gain, tail)


def in_hbm(array):
    return pltpu.with_memory_space_constraint(array, pltpu.HBM)


def in_vmem(array):
    return pltpu.with_memory_space_constraint(array, pltpu.VMEM)


def stage(weights, after=None):
    weights = [(array, first, end) for array, first, end in weights if end > first]
    if not weights:
        return []
    spans = [(first, end) for _, first, end in weights]
    extra = [] if after is None else [after]

    def kernel(*refs):
        inputs, outs, sems = refs[: len(spans)], refs[len(spans) + len(extra) : -1], refs[-1]
        copies = []
        for source, target, (first, end) in zip(inputs, outs, spans):
            for e in range(end - first):
                copies.append(pltpu.make_async_copy(source.at[first + e], target.at[e], sems.at[len(copies)]))
        for copy in copies:
            copy.start()
        for copy in copies:
            copy.wait()

    count = sum(end - first for first, end in spans)
    nbytes = sum((end - first) * array[0].size * 2 for array, first, end in weights)
    copies = pl.pallas_call(
        kernel,
        out_shape=[pltpu.VMEM((end - first, *array.shape[1:]), array.dtype) for array, first, end in weights],
        in_specs=[HBM] * len(spans) + [ANY] * len(extra),
        out_specs=[VMEM] * len(spans),
        scratch_shapes=[pltpu.SemaphoreType.DMA((count,))],
        compiler_params=pltpu.CompilerParams(vmem_limit_bytes=MIB),
        cost_estimate=pl.CostEstimate(flops=0, bytes_accessed=nbytes, transcendentals=0),
        name="stage",
    )(*[in_hbm(array) for array, _, _ in weights], *extra)
    return list(copies)


def shift_of(count):
    return count.bit_length() - 1


def canonical(position, where_ref, sizes):
    reqs, groups, rows = sizes
    req = (position >> shift_of(rows)) & (reqs - 1)
    if reqs <= 4:
        req = req ^ where_ref[1]
    group = (position >> shift_of(rows * reqs)) ^ where_ref[2]
    return (((req << shift_of(groups)) | group) << shift_of(rows)) | (position & (rows - 1))


def pack(place, rows_ref, out_ref):
    width = rows_ref.shape[1]
    chunk = width // CUTS

    def cut(k, carry):
        part = pl.ds(pl.multiple_of(k * chunk, 128), chunk)
        out_ref[:, part] = jnp.dot(place, rows_ref[:, part], preferred_element_type=jnp.float32).astype(jnp.bfloat16)
        return carry

    lax.fori_loop(0, CUTS, cut, 0)


def route_kernel(sizes, top, pieces, where_ref, *refs):
    here = refs[:pieces]
    packed_ref, place_ref, table_ref, rows_ref = refs[pieces:]
    each, half = here[0].shape[0], here[0].shape[1] - TAIL
    experts, _, slots = table_ref.shape
    tokens = each * pieces
    for q in range(pieces):
        rows_ref[q * each : (q + 1) * each, :] = here[q][:, :half]
    tail = jnp.concatenate([ref[:, half:] for ref in here], axis=0).astype(jnp.float32)
    first = where_ref[1] * experts
    lane = lax.broadcasted_iota(jnp.int32, (tokens, TAIL), 1)
    gates = sum(pltpu.roll(tail, TAIL - top * part, 1) for part in (1, 2, 3))
    names = jnp.where(lane < top, tail, -1.0).astype(jnp.int32)
    present = jnp.zeros((tokens, TAIL), jnp.float32)
    weights = []
    for e in range(experts):
        named = names == first + e
        hit = jnp.sum(jnp.where(named, 1.0, 0.0), axis=1, keepdims=True)
        weights.append(jnp.sum(jnp.where(named, gates, 0.0), axis=1, keepdims=True))
        present = jnp.where(lane == e, hit, present)
    token = canonical(lax.broadcasted_iota(jnp.int32, (tokens, tokens), 0), where_ref, sizes)
    other = canonical(lax.broadcasted_iota(jnp.int32, (tokens, tokens), 1), where_ref, sizes)
    earlier = jnp.where(other < token, 1.0, 0.0).astype(jnp.bfloat16)
    rank = jnp.dot(earlier, present.astype(jnp.bfloat16), preferred_element_type=jnp.float32)
    rank = jnp.where(present > 0.0, rank, -1.0)
    token = canonical(lax.broadcasted_iota(jnp.int32, (tokens, 1), 0), where_ref, sizes).astype(jnp.float32)
    slot = lax.broadcasted_iota(jnp.int32, (tokens, slots), 1).astype(jnp.float32)
    for e in range(experts):
        column = jnp.sum(jnp.where(lane == e, rank, 0.0), axis=1, keepdims=True)
        used = slot == column
        table_ref[e, 0:1, :] = jnp.sum(jnp.where(used, weights[e], 0.0), axis=0, keepdims=True)
        table_ref[e, 1:2, :] = jnp.sum(jnp.where(used, token, 0.0), axis=0, keepdims=True)
        place_ref[e * slots : (e + 1) * slots, :] = jnp.where(used, 1.0, 0.0).T.astype(jnp.bfloat16)
    pack(place_ref[...], rows_ref, packed_ref)


def route(where, here, experts, sizes, top):
    pieces = len(here)
    each, half = here[0].shape[0], here[0].shape[1] - TAIL
    tokens = pieces * each
    slots = tokens // sizes[2] * CAP

    def kernel(*refs):
        route_kernel(sizes, top, pieces, *refs)

    nbytes = 2 * tokens * (half + 2 * TAIL) + 2 * experts * slots * (half // 2 + tokens) + 8 * tokens * (tokens + slots)
    return pl.pallas_call(
        kernel,
        out_shape=(
            jax.ShapeDtypeStruct((experts * slots, half), jnp.bfloat16),
            jax.ShapeDtypeStruct((experts * slots, tokens), jnp.bfloat16),
            jax.ShapeDtypeStruct((experts, 8, slots), jnp.float32),
        ),
        in_specs=[SMEM] + [VMEM] * pieces,
        out_specs=(VMEM, VMEM, VMEM),
        scratch_shapes=[pltpu.VMEM((tokens, half), jnp.bfloat16)],
        compiler_params=pltpu.CompilerParams(vmem_limit_bytes=2 * nbytes + 8 * MIB),
        cost_estimate=pl.CostEstimate(
            flops=2 * experts * slots * tokens * half, bytes_accessed=4 * experts * slots * half, transcendentals=0
        ),
        name="route",
    )(where, *here)


def in_order(copies):
    for copy in copies[:FLIGHT]:
        copy.start()

    def wait(index):
        copies[index].wait()
        if index + FLIGHT < len(copies):
            copies[index + FLIGHT].start()

    return wait


def hidden_units(where, place, packed, there, gate_held, up_weight):
    experts, features, units = up_weight.shape
    half = packed.shape[1]
    slots = packed.shape[0] // experts
    depth = min(RING, experts)
    pieces = len(there)
    tokens = place.shape[1]
    each = tokens // pieces

    def kernel(where_ref, place_ref, packed_ref, *refs):
        there_refs, refs = refs[:pieces], refs[pieces:]
        gate_refs, refs = refs[: len(gate_held)], refs[len(gate_held) :]
        up_ref, out_ref, ring_ref, rows_ref, other_ref, ring_sems, sems = refs
        gate_at = [(ref, e) for ref in gate_refs for e in range(ref.shape[0])]
        mine = pl.ds(pl.multiple_of(where_ref[0] * half, 128), half)
        others = pl.ds(pl.multiple_of((1 - where_ref[0]) * half, 128), half)
        wait = in_order([
            pltpu.make_async_copy(
                up_ref.at[e, rows, :], ring_ref.at[e % depth, rows, :], ring_sems.at[2 * (e % depth) + side]
            )
            for e in range(experts)
            for side, rows in enumerate((mine, others))
        ])
        copies = []
        for q in range(pieces):
            span = pl.ds(q * each, each)
            source = there_refs[q].at[:, pl.ds(0, half)]
            copies.append(pltpu.make_async_copy(source, rows_ref.at[span, :], sems.at[q]))
        for copy in copies:
            copy.start()
        for copy in copies:
            copy.wait()
        pack(place_ref[...], rows_ref, other_ref)
        for e in range(experts):
            span = slice(e * slots, (e + 1) * slots)
            gate_ref, index = gate_at[e]
            slot = e % depth
            gate_act = jnp.dot(packed_ref[span, :], gate_ref[index, mine, :], preferred_element_type=jnp.float32)
            gate_act += jnp.dot(other_ref[span, :], gate_ref[index, others, :], preferred_element_type=jnp.float32)
            wait(2 * e)
            up_act = jnp.dot(packed_ref[span, :], ring_ref[slot, mine, :], preferred_element_type=jnp.float32)
            wait(2 * e + 1)
            up_act += jnp.dot(other_ref[span, :], ring_ref[slot, others, :], preferred_element_type=jnp.float32)
            out_ref[e] = (gate_act / (1.0 + jnp.exp(-gate_act)) * up_act).astype(jnp.bfloat16)

    scratch = depth * features * units * 2 + tokens * half * 2 + experts * slots * half * 2
    work = 4 * experts * slots * half // CUTS + 24 * slots * units + 2 * slots * features
    return pl.pallas_call(
        kernel,
        out_shape=jax.ShapeDtypeStruct((experts, slots, units), jnp.bfloat16),
        in_specs=[SMEM, VMEM, VMEM] + [ANY] * pieces + [VMEM] * len(gate_held) + [HBM],
        out_specs=VMEM,
        scratch_shapes=[
            pltpu.VMEM((depth, features, units), jnp.bfloat16),
            pltpu.VMEM((tokens, half), jnp.bfloat16),
            pltpu.VMEM((experts * slots, half), jnp.bfloat16),
            pltpu.SemaphoreType.DMA((2 * depth,)),
            pltpu.SemaphoreType.DMA((pieces,)),
        ],
        compiler_params=pltpu.CompilerParams(vmem_limit_bytes=scratch + work + MIB),
        cost_estimate=pl.CostEstimate(
            flops=4 * experts * slots * features * units,
            bytes_accessed=2 * experts * features * units,
            transcendentals=experts * slots * units,
        ),
        name="gate_up",
    )(where, place, packed, *there, *map(in_vmem, gate_held), in_hbm(up_weight))


def down(where, table, here, there, down_held, tokens):
    reqs = lax.axis_size("req")
    experts, hidden, width = down_held.shape
    _, slots, part = here[0].shape
    pieces = len(here)
    share = tokens if reqs > 4 else tokens // reqs
    shapes = [jax.ShapeDtypeStruct((share, width), jnp.bfloat16)] * (tokens // share)

    def kernel(where_ref, table_ref, *refs):
        here_refs, there_refs, refs = refs[:pieces], refs[pieces : 2 * pieces], refs[2 * pieces :]
        down_ref, outs, (units_ref, acc_ref, sems) = refs[0], refs[1:-3], refs[-3:]
        copies = []
        for q in range(pieces):
            for side, source in ((0, here_refs[q]), (1, there_refs[q])):
                owner = (where_ref[0] ^ side) * pieces + (where_ref[2] ^ q)
                columns = pl.ds(pl.multiple_of(owner * part, 128), part)
                copies.append(pltpu.make_async_copy(source, units_ref.at[:, :, columns], sems.at[2 * q + side]))
        for copy in copies:
            copy.start()
        for copy in copies:
            copy.wait()
        token = lax.broadcasted_iota(jnp.int32, (tokens, slots), 0)
        for e in range(experts):
            projected = jnp.dot(units_ref[e], down_ref[e], preferred_element_type=jnp.float32).astype(jnp.bfloat16)
            named = token == table_ref[e, 1:2, :].astype(jnp.int32)
            weights = jnp.where(named, table_ref[e, 0:1, :], 0.0)
            upper = weights.astype(jnp.bfloat16)
            lower = (weights - upper.astype(jnp.float32)).astype(jnp.bfloat16)
            combined = jnp.dot(upper, projected, preferred_element_type=jnp.float32)
            combined += jnp.dot(lower, projected, preferred_element_type=jnp.float32)
            if e == 0:
                acc_ref[...] = combined
            else:
                acc_ref[...] += combined
        if len(outs) == 1:
            outs[0][...] = acc_ref[...].astype(jnp.bfloat16)
        else:
            for bits, out in enumerate(outs):
                start = pl.multiple_of((where_ref[1] ^ bits) * share, share)
                out[...] = acc_ref[pl.ds(start, share), :].astype(jnp.bfloat16)

    scratch = experts * slots * hidden * 2 + tokens * width * 4
    work = tokens * (slots * 16 + width * 12) + slots * width * 8
    return pl.pallas_call(
        kernel,
        out_shape=shapes,
        in_specs=[SMEM, VMEM] + [ANY] * (2 * pieces) + [VMEM],
        out_specs=[VMEM] * len(shapes),
        scratch_shapes=[
            pltpu.VMEM((experts, slots, hidden), jnp.bfloat16),
            pltpu.VMEM((tokens, width), jnp.float32),
            pltpu.SemaphoreType.DMA((2 * pieces,)),
        ],
        compiler_params=pltpu.CompilerParams(vmem_limit_bytes=scratch + work + 2 * MIB),
        cost_estimate=pl.CostEstimate(
            flops=2 * experts * slots * hidden * width,
            bytes_accessed=2 * experts * hidden * width,
            transcendentals=0,
        ),
        name="down",
    )(where, table, *here, *there, in_vmem(down_held))


def sum_over_req(where, parts, groups, rows):
    width = parts[0].shape[-1]

    def kernel(where_ref, *refs):
        inputs, outs, acc_ref = refs[: len(parts)], refs[len(parts) : -1], refs[-1]
        total = None
        for part in inputs:
            for block in range(part.shape[0]):
                value = part[block].astype(jnp.float32)
                total = value if total is None else total + value
        acc_ref[...] = total
        for bits, out in enumerate(outs):
            start = pl.multiple_of((where_ref[2] ^ bits) * rows, rows)
            out[...] = acc_ref[pl.ds(start, rows), :].astype(jnp.bfloat16)

    return pl.pallas_call(
        kernel,
        out_shape=[jax.ShapeDtypeStruct((rows, width), jnp.bfloat16)] * groups,
        in_specs=[SMEM] + [VMEM] * len(parts),
        out_specs=[VMEM] * groups,
        scratch_shapes=[pltpu.VMEM((groups * rows, width), jnp.float32)],
        compiler_params=pltpu.CompilerParams(vmem_limit_bytes=8 * MIB),
        name="sum_req",
    )(where, *parts)


def mix(where, hidden, parts):
    def kernel(where_ref, hidden_ref, *refs):
        out_ref = refs[-1]
        for bits, part in enumerate(refs[:-1]):
            width = part.shape[1]
            columns = pl.ds(pl.multiple_of((where_ref[2] ^ bits) * width, 128), width)
            out_ref[:, columns] = (hidden_ref[:, columns] + part[...].astype(jnp.float32)).astype(jnp.bfloat16)

    return pl.pallas_call(
        kernel,
        out_shape=jax.ShapeDtypeStruct(hidden.shape, jnp.bfloat16),
        in_specs=[SMEM, VMEM] + [VMEM] * len(parts),
        out_specs=VMEM,
        compiler_params=pltpu.CompilerParams(vmem_limit_bytes=4 * MIB),
        name="mix",
    )(where, hidden, *parts)


def on_device(residual, attn_part, norm_gain, routes, gates, gate_weight, up_weight, down_weight):
    reqs, groups = lax.axis_size("req"), lax.axis_size("grp")
    rows, top = routes.shape
    tokens = reqs * groups * rows
    spots = [lax.axis_index(axis) for axis in ("head", "req", "grp")]
    where = jnp.stack(spots).astype(jnp.int32)
    experts = gate_weight.shape[0]
    attn = attn_part[0]
    there = [swap(attn, "head", 1), swap(residual, "head", 1)]
    base, tail, gain = prepare(where, attn, residual, routes, gates, norm_gain[None, :])
    there, base, tail, gain = lax.optimization_barrier((there, base, tail, gain))
    hidden, packet = norm(where, base, there[0], there[1], gain, tail)

    early = experts * 3 // 8
    first = stage([(gate_weight, 0, early)], packet)
    column, first = gather_rows(packet, "req", first)
    second = stage([(gate_weight, early, experts)], column)
    here = [column] + [swap(column, "grp", bits) for bits in range(1, groups)]
    here, second = lax.optimization_barrier((here, second))
    there = [swap(piece, "head", 1) for piece in here]
    packed, place, table = route(where, here, experts, (reqs, groups, rows), top)
    units = hidden_units(where, place, packed, there, first + second, up_weight)

    held = stage([(down_weight, 0, experts)], units)
    here = [units] + [swap(units, "grp", bits) for bits in range(1, groups)]
    here, held = lax.optimization_barrier((here, held))
    there = [swap(piece, "head", 1) for piece in here]
    partial = down(where, table, here, there, held[0], tokens)

    if reqs > 4:
        parts = partial[0].reshape(reqs, groups * rows, -1)
        parts = [lax.all_to_all(parts, "req", split_axis=0, concat_axis=0, tiled=True)]
    else:
        parts = [partial[0]] + [swap(partial[bits], "req", bits) for bits in range(1, reqs)]
        parts = [part[None] for part in parts]
    sums = sum_over_req(where, parts, groups, rows)
    sums = [sums[0]] + [swap(sums[bits], "grp", bits) for bits in range(1, groups)]
    return mix(where, hidden, sums)


def solution(mesh):
    placed = (
        P(("req", "grp"), "head"),
        P("head", ("req", "grp"), None),
        P("head"),
        P(("req", "grp"), None),
        P(("req", "grp"), None),
        P("req", None, ("head", "grp")),
        P("req", None, ("head", "grp")),
        P("req", None, ("head", "grp")),
    )
    return jax.shard_map(
        on_device, mesh=mesh, in_specs=placed, out_specs=P(("req", "grp"), "head"), check_vma=False
    )
```

time: 285 us -> 92.8 us (0.33)
  waiting for transfers between devices: 153 us -> 16.2 us
  Pallas kernels: 0 us -> 51.4 us
  matrix products: 48.7 us -> 0 us
  blocking collectives: 46.5 us -> 0 us
  starting transfers between devices: 4.72 us -> 23.3 us
  local copies, waits for them, and re-layouts: 15.8 us -> 1.33 us
  between operations: 13.2 us -> 0.17 us
    all_gather x3 -> x0, waiting for transfers between devices: 120 us -> none  [the longest x1 81.9 us: on_device(): lax.all_gather(whole_rows[None], 'grp', axis=0, tiled=True)]
    pallas_call x0 -> x11, Pallas kernels: none -> 51.4 us  [the longest x3 20 us: stage(): pl.pallas_call(kernel, out_shape=[pltpu.VMEM((end - first, *array.shape[1...]
    dot_general x5 -> x0, matrix products: 48.7 us -> none  [the longest x1 15.8 us: expert_hidden(): jnp.einsum('gresd,edf->gresf', shaped, up_weight, preferred_element_type=...]
    all_to_all x2 -> x0, blocking collectives: 44 us -> none  [the longest x1 28.1 us: on_device(): lax.all_to_all(packed, 'req', split_axis=0, concat_axis=0, tiled=True)]
    ppermute x0 -> x25, starting transfers between devices: none -> 23.3 us  [swap(): lax.ppermute(array, axis, [(i, i ^ bits) for i in range(lax.axis_size(axi...]
    all_to_all x1 -> x0, waiting for transfers between devices: 21.9 us -> none  [on_device(): lax.all_to_all(regrouped, 'req', split_axis=0, concat_axis=0, tiled=True)]
    ppermute x0 -> x25, waiting for transfers between devices: none -> 16.2 us  [swap(): lax.ppermute(array, axis, [(i, i ^ bits) for i in range(lax.axis_size(axi...]
    reshape x3 -> x0, local copies, waits for them, and re-layouts: 14 us -> none  [the longest x1 12.6 us: expert_hidden(): arrived.reshape(groups, sources, local_experts, columns // local_experts,...]
  transfers between devices with their start and end apart: 5 -> 25, of which waited for: 5 -> 13; matrix products, arithmetic and copies ran while one was open for 1% -> 2% of each run, Pallas kernels for 0% -> 27%
where the time goes in v1:
time: 92.8 us; the launch traced here: 92.5 us
  Pallas kernels  51.4 us (55%)
  starting transfers between devices  23.3 us (25%)
  waiting for transfers between devices  16.2 us (17%)
  local copies, waits for them, and re-layouts  1.33 us (1%)
    ppermute x25, starting transfers between devices, swap(): lax.ppermute(array, axis, [(i, i ^ bits) for i in range(lax.axis_size(axi...  23.3 us
    pallas_call x3, Pallas kernels, stage(): pl.pallas_call(kernel, out_shape=[pltpu.VMEM((end - first, *array.shape[1...  20 us
    pallas_call x1, Pallas kernels, hidden_units(): pl.pallas_call(kernel, out_shape=jax.ShapeDtypeStruct((experts, slots, un...  16.4 us
    ppermute x25, waiting for transfers between devices, swap(): lax.ppermute(array, axis, [(i, i ^ bits) for i in range(lax.axis_size(axi...  16.2 us
    pallas_call x1, Pallas kernels, down(): pl.pallas_call(kernel, out_shape=shapes, in_specs=[SMEM, VMEM] + [ANY] *...  7.38 us
    pallas_call x1, Pallas kernels, route(): pl.pallas_call(kernel, out_shape=(jax.ShapeDtypeStruct((experts * slots,...  3.51 us
  transfers between devices with their start and end apart: 25, of which 13 were waited for; matrix products, arithmetic and copies ran while one was open for 2% of the time, Pallas kernels for 27%

profile of v1, /device:TPU:0, one launch (start us, length us, event | category | flops | bytes accessed | tf_op | source)
XLA Modules:
  0.0 92.5 jit_solution(6890179001920683653)
XLA Ops:
  0.0 0.5 collective-permute-start
  0.5 0.1 collective-permute-start.1
  0.5 1.3 %broadcast_in_dim.15.refs_4_ = f32[1,3584]{1,0:T(1,128)} reshape(f32[3584]{0:T(1024)} %param.10) | data formatting | bytes 28672 | tf_op jit(solution)/shard_map/broadcast_in_dim | solution.py:446
  1.8 0.1 pad_add_fusion.where_ref.refs_0_
  1.9 1.6 %prepare.1 = (f32[8,7168]{1,0:T(8,128)S(1)}, bf16[8,128]{1,0:T(8,128)(2,1)S(1)}, f32[1,3584]{1,0:T(1,128)S(1)}) custom-call(s32[3]{0:T(128)S(1)} %pad_add_fusion.where_ref.refs_0_, bf16[8,7168]{1,0:T(8,128)(2,1)} %bitcast.13, bf16[8,3584]{1,0:T(8,128)(2,1)} %refs_1_.1, s32[8,8]{1,0:T(8,128)} %refs_2_.1, f32[8,8]{1,0:T(8,128)} %refs_3_.1, ...), custom_call_target="tpu_custom_call" | custom-call | tf_op jit(solution)/shard_map/prepare/pallas_call | solution.py:75
  3.5 0.0 collective-permute-done.1.res_there_ref
  3.5 0.7 norm.1
  4.2 3.1 %collective-permute-start.2 = (bf16[8,3712]{1,0:T(8,128)(2,1)S(1)}, bf16[8,3712]{1,0:T(8,128)(2,1)S(1)}, u32[]{:S(2)}, u32[]{:S(2)}) collective-permute-start(bf16[8,3712]{1,0:T(8,128)(2,1)S(1)} %get-tuple-element.51.refs_1_.refs_0_), channel_id=1, source_target_pairs={{0,8},{8,0},{16,24},{24,16},{1,9},{9,1},{17,25},{25,17},{2,10},{10... | collective-permute-start | bytes 178184 | tf_op jit(solution)/shard_map/ppermute | solution.py:22
  7.3 2.6 %collective-permute-start.3 = (bf16[8,3712]{1,0:T(8,128)(2,1)S(1)}, bf16[8,3712]{1,0:T(8,128)(2,1)S(1)}, u32[]{:S(2)}, u32[]{:S(2)}) collective-permute-start(bf16[8,3712]{1,0:T(8,128)(2,1)S(1)} %get-tuple-element.51.refs_1_.refs_0_), channel_id=1, source_target_pairs={{0,16},{8,24},{16,0},{24,8},{1,17},{9,25},{17,1},{25,9},{2,18},{10... | collective-permute-start | bytes 178184 | tf_op jit(solution)/shard_map/ppermute | solution.py:22
  9.9 4.2 %stage.3.refs_4_ = bf16[3,7168,256]{2,1,0:T(8,128)(2,1)S(1)} custom-call(bf16[8,7168,256]{2,1,0:T(8,128)(2,1)} %refs_0_.4, bf16[8,3712]{1,0:T(8,128)(2,1)S(1)} %get-tuple-element.51.refs_1_.refs_0_), custom_call_target="tpu_custom_call" | custom-call | bytes 11010048 | tf_op jit(solution)/shard_map/stage/pallas_call | solution.py:147
  14.2 1.7 %collective-permute-done.4.refs_3_ = bf16[8,3712]{1,0:T(8,128)(2,1)S(1)} collective-permute-done((bf16[8,3712]{1,0:T(8,128)(2,1)S(1)}, bf16[8,3712]{1,0:T(8,128)(2,1)S(1)}, u32[]{:S(2)}, u32[]{:S(2)}) %collective-permute-start.4) | collective-permute-done | bytes 59424 | tf_op jit(solution)/shard_map/ppermute | solution.py:22
  16.0 1.6 %collective-permute-start.5 = (bf16[32,3712]{1,0:T(8,128)(2,1)S(1)}, bf16[32,3712]{1,0:T(8,128)(2,1)S(1)}, u32[]{:S(2)}, u32[]{:S(2)}) collective-permute-start(bf16[32,3712]{1,0:T(8,128)(2,1)S(1)} %collect.1.refs_1_), channel_id=1, source_target_pairs={{0,1},{1,0},{2,3},{3,2},{4,5},{5,4},{6,7},{7,6},{8,9},{9,8},{10,11... | collective-permute-start | bytes 712712 | tf_op jit(solution)/shard_map/ppermute | solution.py:22
  17.5 1.5 %collective-permute-start.6 = (bf16[32,3712]{1,0:T(8,128)(2,1)S(1)}, bf16[32,3712]{1,0:T(8,128)(2,1)S(1)}, u32[]{:S(2)}, u32[]{:S(2)}) collective-permute-start(bf16[32,3712]{1,0:T(8,128)(2,1)S(1)} %collect.1.refs_1_), channel_id=1, source_target_pairs={{0,2},{1,3},{2,0},{3,1},{4,6},{5,7},{6,4},{7,5},{8,10},{9,11},{10,... | collective-permute-start | bytes 712712 | tf_op jit(solution)/shard_map/ppermute | solution.py:22
  19.0 0.5 collective-permute-start.7
  19.5 6.3 %stage.4.refs_5_ = bf16[5,7168,256]{2,1,0:T(8,128)(2,1)S(1)} custom-call(bf16[8,7168,256]{2,1,0:T(8,128)(2,1)} %refs_0_.4, bf16[32,3712]{1,0:T(8,128)(2,1)S(1)} %collect.1.refs_1_), custom_call_target="tpu_custom_call" | custom-call | bytes 18350080 | tf_op jit(solution)/shard_map/stage/pallas_call | solution.py:147
  25.9 2.5 %collective-permute-done.6.refs_3_ = bf16[32,3712]{1,0:T(8,128)(2,1)S(1)} collective-permute-done((bf16[32,3712]{1,0:T(8,128)(2,1)S(1)}, bf16[32,3712]{1,0:T(8,128)(2,1)S(1)}, u32[]{:S(2)}, u32[]{:S(2)}) %collective-permute-start.6) | collective-permute-done | bytes 237600 | tf_op jit(solution)/shard_map/ppermute | solution.py:22
  28.4 0.5 collective-permute-start.9
  28.9 0.0 collective-permute-start.10
  28.9 0.5 collective-permute-start.11
  29.4 3.5 %route.1 = (bf16[512,3584]{1,0:T(8,128)(2,1)S(1)}, bf16[512,128]{1,0:T(8,128)(2,1)S(1)}, f32[8,8,64]{2,1,0:T(8,128)S(1)}) custom-call(s32[3]{0:T(128)S(1)} %pad_add_fusion.where_ref.refs_0_, bf16[32,3712]{1,0:T(8,128)(2,1)S(1)} %collect.1.refs_1_, bf16[32,3712]{1,0:T(8,128)(2,1)S(1)} %collective-permute-done.5.refs_2_, ...), custom_call_target="tpu_custom_call" | custom-call | flops 469762048 | bytes 7340032 | tf_op jit(solution)/shard_map/route/pallas_call | solution.py:231
  33.0 16.4 %gate_up.1.refs_1_.refs_0_ = bf16[8,64,256]{2,1,0:T(8,128)(2,1)S(1)} custom-call(s32[3]{0:T(128)S(1)} %pad_add_fusion.where_ref.refs_0_, bf16[512,128]{1,0:T(8,128)(2,1)S(1)} %get-tuple-element.60.place_ref, bf16[512,3584]{1,0:T(8,128)(2,1)S(1)} %get-tuple-element.61.packed_ref, bf16[32,3712]{1,0:T(8,128)(2,1)S(1)} %collective-permute-done.8.refs_0_, ...), custom_call_target="tpu_custom_call" | custom-call | flops 3758096384 | bytes 29360128 | tf_op jit(solution)/shard_map/gate_up/pallas_call | solution.py:308
  49.4 1.3 %collective-permute-start.12 = (bf16[8,64,256]{2,1,0:T(8,128)(2,1)S(1)}, bf16[8,64,256]{2,1,0:T(8,128)(2,1)S(1)}, u32[]{:S(2)}, u32[]{:S(2)}) collective-permute-start(bf16[8,64,256]{2,1,0:T(8,128)(2,1)S(1)} %gate_up.1.refs_1_.refs_0_), channel_id=1, source_target_pairs={{0,1},{1,0},{2,3},{3,2},{4,5},{5,4},{6,7},{7,6},{8,9},{9,8},{10,11... | collective-permute-start | bytes 786440 | tf_op jit(solution)/shard_map/ppermute | solution.py:22
  50.7 0.8 collective-permute-start.13
  51.5 1.4 %collective-permute-start.14 = (bf16[8,64,256]{2,1,0:T(8,128)(2,1)S(1)}, bf16[8,64,256]{2,1,0:T(8,128)(2,1)S(1)}, u32[]{:S(2)}, u32[]{:S(2)}) collective-permute-start(bf16[8,64,256]{2,1,0:T(8,128)(2,1)S(1)} %gate_up.1.refs_1_.refs_0_), channel_id=1, source_target_pairs={{0,3},{1,2},{2,1},{3,0},{4,7},{5,6},{6,5},{7,4},{8,11},{9,10},{10,... | collective-permute-start | bytes 786440 | tf_op jit(solution)/shard_map/ppermute | solution.py:22
  52.9 9.5 %stage.5.refs_8_ = bf16[8,2048,896]{2,1,0:T(8,128)(2,1)S(1)} custom-call(bf16[8,2048,896]{2,1,0:T(8,128)(2,1)} %refs_0_.5, bf16[8,64,256]{2,1,0:T(8,128)(2,1)S(1)} %gate_up.1.refs_1_.refs_0_), custom_call_target="tpu_custom_call" | custom-call | bytes 29360128 | tf_op jit(solution)/shard_map/stage/pallas_call | solution.py:147
  62.4 0.2 collective-permute-done.13.refs_2_
  62.6 1.6 %collective-permute-done.14.refs_3_ = bf16[8,64,256]{2,1,0:T(8,128)(2,1)S(1)} collective-permute-done((bf16[8,64,256]{2,1,0:T(8,128)(2,1)S(1)}, bf16[8,64,256]{2,1,0:T(8,128)(2,1)S(1)}, u32[]{:S(2)}, u32[]{:S(2)}) %collective-permute-start.14) | collective-permute-done | bytes 262176 | tf_op jit(solution)/shard_map/ppermute | solution.py:22
  64.2 0.5 collective-permute-start.16
  64.7 0.0 collective-permute-start.17
  64.7 0.5 collective-permute-start.18
  65.2 0.5 collective-permute-done.15.refs_4_
  65.8 0.4 collective-permute-done.16.refs_5_
  66.1 0.4 collective-permute-done.17.refs_6_
  66.5 0.4 collective-permute-done.18.refs_7_
  66.9 7.4 %down.1 = (bf16[32,896]{1,0:T(8,128)(2,1)S(1)}, bf16[32,896]{1,0:T(8,128)(2,1)S(1)}, bf16[32,896]{1,0:T(8,128)(2,1)S(1)}, bf16[32,896]{1,0:T(8,128)(2,1)S(1)}) custom-call(s32[3]{0:T(128)S(1)} %pad_add_fusion.where_ref.refs_0_, f32[8,8,64]{2,1,0:T(8,128)S(1)} %get-tuple-element.59.table_ref, bf16[8,64,256]{2,1,0:T(8,128)(2,1)S(1)} %gate_up.1.refs_1_.refs_0_, ...), custom_call_target="tpu_custom_call" | custom-call | flops 1879048192 | bytes 29360128 | tf_op jit(solution)/shard_map/down/pallas_call | solution.py:373
  74.3 0.3 collective-permute-start.19
  74.5 3.2 %collective-permute-start.20 = (bf16[32,896]{1,0:T(8,128)(2,1)S(1)}, bf16[32,896]{1,0:T(8,128)(2,1)S(1)}, u32[]{:S(2)}, u32[]{:S(2)}) collective-permute-start(bf16[32,896]{1,0:T(8,128)(2,1)S(1)} %get-tuple-element.71), channel_id=1, source_target_pairs={{0,16},{8,24},{16,0},{24,8},{1,17},{9,25},{17,1},{25,9},{2,18},{10... | collective-permute-start | bytes 172040 | tf_op jit(solution)/shard_map/ppermute | solution.py:22
  77.8 1.0 %collective-permute-start.21 = (bf16[32,896]{1,0:T(8,128)(2,1)S(1)}, bf16[32,896]{1,0:T(8,128)(2,1)S(1)}, u32[]{:S(2)}, u32[]{:S(2)}) collective-permute-start(bf16[32,896]{1,0:T(8,128)(2,1)S(1)} %get-tuple-element.72), channel_id=1, source_target_pairs={{0,24},{8,16},{16,8},{24,0},{1,25},{9,17},{17,9},{25,1},{2,26},{10... | collective-permute-start | bytes 172040 | tf_op jit(solution)/shard_map/ppermute | solution.py:22
  78.7 2.7 %collective-permute-done.20 = bf16[32,896]{1,0:T(8,128)(2,1)S(1)} collective-permute-done((bf16[32,896]{1,0:T(8,128)(2,1)S(1)}, bf16[32,896]{1,0:T(8,128)(2,1)S(1)}, u32[]{:S(2)}, u32[]{:S(2)}) %collective-permute-start.20) | collective-permute-done | bytes 57376 | tf_op jit(solution)/shard_map/ppermute | solution.py:22
  81.5 2.3 %collective-permute-done.21 = bf16[32,896]{1,0:T(8,128)(2,1)S(1)} collective-permute-done((bf16[32,896]{1,0:T(8,128)(2,1)S(1)}, bf16[32,896]{1,0:T(8,128)(2,1)S(1)}, u32[]{:S(2)}, u32[]{:S(2)}) %collective-permute-start.21) | collective-permute-done | bytes 57376 | tf_op jit(solution)/shard_map/ppermute | solution.py:22
  83.7 0.6 sum_req.1
  84.3 0.8 collective-permute-start.22
  85.2 1.5 %collective-permute-start.23 = (bf16[8,896]{1,0:T(8,128)(2,1)S(1)}, bf16[8,896]{1,0:T(8,128)(2,1)S(1)}, u32[]{:S(2)}, u32[]{:S(2)}) collective-permute-start(bf16[8,896]{1,0:T(8,128)(2,1)S(1)} %get-tuple-element.75), channel_id=1, source_target_pairs={{0,2},{1,3},{2,0},{3,1},{4,6},{5,7},{6,4},{7,5},{8,10},{9,11},{10,... | collective-permute-start | bytes 43016 | tf_op jit(solution)/shard_map/ppermute | solution.py:22
  86.7 1.2 %collective-permute-start.24 = (bf16[8,896]{1,0:T(8,128)(2,1)S(1)}, bf16[8,896]{1,0:T(8,128)(2,1)S(1)}, u32[]{:S(2)}, u32[]{:S(2)}) collective-permute-start(bf16[8,896]{1,0:T(8,128)(2,1)S(1)} %get-tuple-element.76), channel_id=1, source_target_pairs={{0,3},{1,2},{2,1},{3,0},{4,7},{5,6},{6,5},{7,4},{8,11},{9,10},{10,... | collective-permute-start | bytes 43016 | tf_op jit(solution)/shard_map/ppermute | solution.py:22
  87.9 0.2 collective-permute-done.22.refs_1_
  88.1 0.8 collective-permute-done.23.refs_2_
  88.9 2.4 %collective-permute-done.24.refs_3_ = bf16[8,896]{1,0:T(8,128)(2,1)S(1)} collective-permute-done((bf16[8,896]{1,0:T(8,128)(2,1)S(1)}, bf16[8,896]{1,0:T(8,128)(2,1)S(1)}, u32[]{:S(2)}, u32[]{:S(2)}) %collective-permute-start.24) | collective-permute-done | bytes 14368 | tf_op jit(solution)/shard_map/ppermute | solution.py:22
  91.3 1.2 %mix.1 = bf16[8,3584]{1,0:T(8,128)(2,1)} custom-call(s32[3]{0:T(128)S(1)} %pad_add_fusion.where_ref.refs_0_, f32[8,3584]{1,0:T(8,128)S(1)} %get-tuple-element.49.hidden_ref, bf16[8,896]{1,0:T(8,128)(2,1)S(1)} %get-tuple-element.73.refs_0_, bf16[8,896]{1,0:T(8,128)(2,1)S(1)} %collective-permute-done.22.refs_1_, ...), custom_call_target="tpu_custom_call" | custom-call | tf_op jit(solution)/shard_map/mix/pallas_call | solution.py:427
  (15 shorter events, 0.1 us)
Async XLA Ops:
  0.0 3.5 %collective-permute-start = (bf16[8,7168]{1,0:T(8,128)(2,1)}, bf16[8,7168]{1,0:T(8,128)(2,1)S(1)}, u32[]{:S(2)}, u32[]{:S(2)}) collective-permute-start(bf16[8,7168]{1,0:T(8,128)(2,1)} %bitcast.12), channel_id=1, source_target_pairs={{0,4},{4,0},{1,5},{5,1},{2,6},{6,2},{3,7},{7,3},{8,12},{12,8},{9,1... | collective-permute-start | bytes 344072 | tf_op jit(solution)/shard_map/ppermute | solution.py:22
  0.5 3.1 %collective-permute-start.1 = (bf16[8,3584]{1,0:T(8,128)(2,1)}, bf16[8,3584]{1,0:T(8,128)(2,1)S(1)}, u32[]{:S(2)}, u32[]{:S(2)}) collective-permute-start(bf16[8,3584]{1,0:T(8,128)(2,1)} %refs_1_.1), channel_id=1, source_target_pairs={{0,4},{4,0},{1,5},{5,1},{2,6},{6,2},{3,7},{7,3},{8,12},{12,8},{9,1... | collective-permute-start | bytes 172040 | tf_op jit(solution)/shard_map/ppermute | solution.py:22
  4.2 9.9 %collective-permute-start.2 = (bf16[8,3712]{1,0:T(8,128)(2,1)S(1)}, bf16[8,3712]{1,0:T(8,128)(2,1)S(1)}, u32[]{:S(2)}, u32[]{:S(2)}) collective-permute-start(bf16[8,3712]{1,0:T(8,128)(2,1)S(1)} %get-tuple-element.51.refs_1_.refs_0_), channel_id=1, source_target_pairs={{0,8},{8,0},{16,24},{24,16},{1,9},{9,1},{17,25},{25,17},{2,10},{10... | collective-permute-start | bytes 178184 | tf_op jit(solution)/shard_map/ppermute | solution.py:22
  7.3 6.8 %collective-permute-start.3 = (bf16[8,3712]{1,0:T(8,128)(2,1)S(1)}, bf16[8,3712]{1,0:T(8,128)(2,1)S(1)}, u32[]{:S(2)}, u32[]{:S(2)}) collective-permute-start(bf16[8,3712]{1,0:T(8,128)(2,1)S(1)} %get-tuple-element.51.refs_1_.refs_0_), channel_id=1, source_target_pairs={{0,16},{8,24},{16,0},{24,8},{1,17},{9,25},{17,1},{25,9},{2,18},{10... | collective-permute-start | bytes 178184 | tf_op jit(solution)/shard_map/ppermute | solution.py:22
  9.9 6.0 %collective-permute-start.4 = (bf16[8,3712]{1,0:T(8,128)(2,1)S(1)}, bf16[8,3712]{1,0:T(8,128)(2,1)S(1)}, u32[]{:S(2)}, u32[]{:S(2)}) collective-permute-start(bf16[8,3712]{1,0:T(8,128)(2,1)S(1)} %get-tuple-element.51.refs_1_.refs_0_), channel_id=1, source_target_pairs={{0,24},{8,16},{16,8},{24,0},{1,25},{9,17},{17,9},{25,1},{2,26},{10... | collective-permute-start | bytes 178184 | tf_op jit(solution)/shard_map/ppermute | solution.py:22
  16.0 9.9 %collective-permute-start.5 = (bf16[32,3712]{1,0:T(8,128)(2,1)S(1)}, bf16[32,3712]{1,0:T(8,128)(2,1)S(1)}, u32[]{:S(2)}, u32[]{:S(2)}) collective-permute-start(bf16[32,3712]{1,0:T(8,128)(2,1)S(1)} %collect.1.refs_1_), channel_id=1, source_target_pairs={{0,1},{1,0},{2,3},{3,2},{4,5},{5,4},{6,7},{7,6},{8,9},{9,8},{10,11... | collective-permute-start | bytes 712712 | tf_op jit(solution)/shard_map/ppermute | solution.py:22
  17.5 10.9 %collective-permute-start.6 = (bf16[32,3712]{1,0:T(8,128)(2,1)S(1)}, bf16[32,3712]{1,0:T(8,128)(2,1)S(1)}, u32[]{:S(2)}, u32[]{:S(2)}) collective-permute-start(bf16[32,3712]{1,0:T(8,128)(2,1)S(1)} %collect.1.refs_1_), channel_id=1, source_target_pairs={{0,2},{1,3},{2,0},{3,1},{4,6},{5,7},{6,4},{7,5},{8,10},{9,11},{10,... | collective-permute-start | bytes 712712 | tf_op jit(solution)/shard_map/ppermute | solution.py:22
  19.0 9.4 %collective-permute-start.7 = (bf16[32,3712]{1,0:T(8,128)(2,1)S(1)}, bf16[32,3712]{1,0:T(8,128)(2,1)S(1)}, u32[]{:S(2)}, u32[]{:S(2)}) collective-permute-start(bf16[32,3712]{1,0:T(8,128)(2,1)S(1)} %collect.1.refs_1_), channel_id=1, source_target_pairs={{0,3},{1,2},{2,1},{3,0},{4,7},{5,6},{6,5},{7,4},{8,11},{9,10},{10,... | collective-permute-start | bytes 712712 | tf_op jit(solution)/shard_map/ppermute | solution.py:22
  28.4 4.5 %collective-permute-start.8 = (bf16[32,3712]{1,0:T(8,128)(2,1)S(1)}, bf16[32,3712]{1,0:T(8,128)(2,1)S(1)}, u32[]{:S(2)}, u32[]{:S(2)}) collective-permute-start(bf16[32,3712]{1,0:T(8,128)(2,1)S(1)} %collect.1.refs_1_), channel_id=1, source_target_pairs={{0,4},{4,0},{1,5},{5,1},{2,6},{6,2},{3,7},{7,3},{8,12},{12,8},{9,1... | collective-permute-start | bytes 712712 | tf_op jit(solution)/shard_map/ppermute | solution.py:22
  28.4 4.6 %collective-permute-start.9 = (bf16[32,3712]{1,0:T(8,128)(2,1)S(1)}, bf16[32,3712]{1,0:T(8,128)(2,1)S(1)}, u32[]{:S(2)}, u32[]{:S(2)}) collective-permute-start(bf16[32,3712]{1,0:T(8,128)(2,1)S(1)} %collective-permute-done.5.refs_2_), channel_id=1, source_target_pairs={{0,4},{4,0},{1,5},{5,1},{2,6},{6,2},{3,7},{7,3},{8,12},{12,8},{9,1... | collective-permute-start | bytes 712712 | tf_op jit(solution)/shard_map/ppermute | solution.py:22
  28.9 4.1 %collective-permute-start.10 = (bf16[32,3712]{1,0:T(8,128)(2,1)S(1)}, bf16[32,3712]{1,0:T(8,128)(2,1)S(1)}, u32[]{:S(2)}, u32[]{:S(2)}) collective-permute-start(bf16[32,3712]{1,0:T(8,128)(2,1)S(1)} %collective-permute-done.6.refs_3_), channel_id=1, source_target_pairs={{0,4},{4,0},{1,5},{5,1},{2,6},{6,2},{3,7},{7,3},{8,12},{12,8},{9,1... | collective-permute-start | bytes 712712 | tf_op jit(solution)/shard_map/ppermute | solution.py:22
  28.9 4.1 %collective-permute-start.11 = (bf16[32,3712]{1,0:T(8,128)(2,1)S(1)}, bf16[32,3712]{1,0:T(8,128)(2,1)S(1)}, u32[]{:S(2)}, u32[]{:S(2)}) collective-permute-start(bf16[32,3712]{1,0:T(8,128)(2,1)S(1)} %collective-permute-done.7.refs_4_), channel_id=1, source_target_pairs={{0,4},{4,0},{1,5},{5,1},{2,6},{6,2},{3,7},{7,3},{8,12},{12,8},{9,1... | collective-permute-start | bytes 712712 | tf_op jit(solution)/shard_map/ppermute | solution.py:22
  49.4 13.1 %collective-permute-start.12 = (bf16[8,64,256]{2,1,0:T(8,128)(2,1)S(1)}, bf16[8,64,256]{2,1,0:T(8,128)(2,1)S(1)}, u32[]{:S(2)}, u32[]{:S(2)}) collective-permute-start(bf16[8,64,256]{2,1,0:T(8,128)(2,1)S(1)} %gate_up.1.refs_1_.refs_0_), channel_id=1, source_target_pairs={{0,1},{1,0},{2,3},{3,2},{4,5},{5,4},{6,7},{7,6},{8,9},{9,8},{10,11... | collective-permute-start | bytes 786440 | tf_op jit(solution)/shard_map/ppermute | solution.py:22
  50.7 11.9 %collective-permute-start.13 = (bf16[8,64,256]{2,1,0:T(8,128)(2,1)S(1)}, bf16[8,64,256]{2,1,0:T(8,128)(2,1)S(1)}, u32[]{:S(2)}, u32[]{:S(2)}) collective-permute-start(bf16[8,64,256]{2,1,0:T(8,128)(2,1)S(1)} %gate_up.1.refs_1_.refs_0_), channel_id=1, source_target_pairs={{0,2},{1,3},{2,0},{3,1},{4,6},{5,7},{6,4},{7,5},{8,10},{9,11},{10,... | collective-permute-start | bytes 786440 | tf_op jit(solution)/shard_map/ppermute | solution.py:22
  51.5 12.7 %collective-permute-start.14 = (bf16[8,64,256]{2,1,0:T(8,128)(2,1)S(1)}, bf16[8,64,256]{2,1,0:T(8,128)(2,1)S(1)}, u32[]{:S(2)}, u32[]{:S(2)}) collective-permute-start(bf16[8,64,256]{2,1,0:T(8,128)(2,1)S(1)} %gate_up.1.refs_1_.refs_0_), channel_id=1, source_target_pairs={{0,3},{1,2},{2,1},{3,0},{4,7},{5,6},{6,5},{7,4},{8,11},{9,10},{10,... | collective-permute-start | bytes 786440 | tf_op jit(solution)/shard_map/ppermute | solution.py:22
  64.2 1.5 %collective-permute-start.15 = (bf16[8,64,256]{2,1,0:T(8,128)(2,1)S(1)}, bf16[8,64,256]{2,1,0:T(8,128)(2,1)S(1)}, u32[]{:S(2)}, u32[]{:S(2)}) collective-permute-start(bf16[8,64,256]{2,1,0:T(8,128)(2,1)S(1)} %gate_up.1.refs_1_.refs_0_), channel_id=1, source_target_pairs={{0,4},{4,0},{1,5},{5,1},{2,6},{6,2},{3,7},{7,3},{8,12},{12,8},{9,1... | collective-permute-start | bytes 786440 | tf_op jit(solution)/shard_map/ppermute | solution.py:22
  64.2 1.9 %collective-permute-start.16 = (bf16[8,64,256]{2,1,0:T(8,128)(2,1)S(1)}, bf16[8,64,256]{2,1,0:T(8,128)(2,1)S(1)}, u32[]{:S(2)}, u32[]{:S(2)}) collective-permute-start(bf16[8,64,256]{2,1,0:T(8,128)(2,1)S(1)} %collective-permute-done.12.refs_1_), channel_id=1, source_target_pairs={{0,4},{4,0},{1,5},{5,1},{2,6},{6,2},{3,7},{7,3},{8,12},{12,8},{9,1... | collective-permute-start | bytes 786440 | tf_op jit(solution)/shard_map/ppermute | solution.py:22
  64.7 1.8 %collective-permute-start.17 = (bf16[8,64,256]{2,1,0:T(8,128)(2,1)S(1)}, bf16[8,64,256]{2,1,0:T(8,128)(2,1)S(1)}, u32[]{:S(2)}, u32[]{:S(2)}) collective-permute-start(bf16[8,64,256]{2,1,0:T(8,128)(2,1)S(1)} %collective-permute-done.13.refs_2_), channel_id=1, source_target_pairs={{0,4},{4,0},{1,5},{5,1},{2,6},{6,2},{3,7},{7,3},{8,12},{12,8},{9,1... | collective-permute-start | bytes 786440 | tf_op jit(solution)/shard_map/ppermute | solution.py:22
  64.7 2.1 %collective-permute-start.18 = (bf16[8,64,256]{2,1,0:T(8,128)(2,1)S(1)}, bf16[8,64,256]{2,1,0:T(8,128)(2,1)S(1)}, u32[]{:S(2)}, u32[]{:S(2)}) collective-permute-start(bf16[8,64,256]{2,1,0:T(8,128)(2,1)S(1)} %collective-permute-done.14.refs_3_), channel_id=1, source_target_pairs={{0,4},{4,0},{1,5},{5,1},{2,6},{6,2},{3,7},{7,3},{8,12},{12,8},{9,1... | collective-permute-start | bytes 786440 | tf_op jit(solution)/shard_map/ppermute | solution.py:22
  74.3 4.5 %collective-permute-start.19 = (bf16[32,896]{1,0:T(8,128)(2,1)S(1)}, bf16[32,896]{1,0:T(8,128)(2,1)S(1)}, u32[]{:S(2)}, u32[]{:S(2)}) collective-permute-start(bf16[32,896]{1,0:T(8,128)(2,1)S(1)} %get-tuple-element.70), channel_id=1, source_target_pairs={{0,8},{8,0},{16,24},{24,16},{1,9},{9,1},{17,25},{25,17},{2,10},{10... | collective-permute-start | bytes 172040 | tf_op jit(solution)/shard_map/ppermute | solution.py:22
  74.5 6.9 %collective-permute-start.20 = (bf16[32,896]{1,0:T(8,128)(2,1)S(1)}, bf16[32,896]{1,0:T(8,128)(2,1)S(1)}, u32[]{:S(2)}, u32[]{:S(2)}) collective-permute-start(bf16[32,896]{1,0:T(8,128)(2,1)S(1)} %get-tuple-element.71), channel_id=1, source_target_pairs={{0,16},{8,24},{16,0},{24,8},{1,17},{9,25},{17,1},{25,9},{2,18},{10... | collective-permute-start | bytes 172040 | tf_op jit(solution)/shard_map/ppermute | solution.py:22
  77.8 6.0 %collective-permute-start.21 = (bf16[32,896]{1,0:T(8,128)(2,1)S(1)}, bf16[32,896]{1,0:T(8,128)(2,1)S(1)}, u32[]{:S(2)}, u32[]{:S(2)}) collective-permute-start(bf16[32,896]{1,0:T(8,128)(2,1)S(1)} %get-tuple-element.72), channel_id=1, source_target_pairs={{0,24},{8,16},{16,8},{24,0},{1,25},{9,17},{17,9},{25,1},{2,26},{10... | collective-permute-start | bytes 172040 | tf_op jit(solution)/shard_map/ppermute | solution.py:22
  84.3 3.8 %collective-permute-start.22 = (bf16[8,896]{1,0:T(8,128)(2,1)S(1)}, bf16[8,896]{1,0:T(8,128)(2,1)S(1)}, u32[]{:S(2)}, u32[]{:S(2)}) collective-permute-start(bf16[8,896]{1,0:T(8,128)(2,1)S(1)} %get-tuple-element.74), channel_id=1, source_target_pairs={{0,1},{1,0},{2,3},{3,2},{4,5},{5,4},{6,7},{7,6},{8,9},{9,8},{10,11... | collective-permute-start | bytes 43016 | tf_op jit(solution)/shard_map/ppermute | solution.py:22
  85.2 3.7 %collective-permute-start.23 = (bf16[8,896]{1,0:T(8,128)(2,1)S(1)}, bf16[8,896]{1,0:T(8,128)(2,1)S(1)}, u32[]{:S(2)}, u32[]{:S(2)}) collective-permute-start(bf16[8,896]{1,0:T(8,128)(2,1)S(1)} %get-tuple-element.75), channel_id=1, source_target_pairs={{0,2},{1,3},{2,0},{3,1},{4,6},{5,7},{6,4},{7,5},{8,10},{9,11},{10,... | collective-permute-start | bytes 43016 | tf_op jit(solution)/shard_map/ppermute | solution.py:22
  86.7 4.6 %collective-permute-start.24 = (bf16[8,896]{1,0:T(8,128)(2,1)S(1)}, bf16[8,896]{1,0:T(8,128)(2,1)S(1)}, u32[]{:S(2)}, u32[]{:S(2)}) collective-permute-start(bf16[8,896]{1,0:T(8,128)(2,1)S(1)} %get-tuple-element.76), channel_id=1, source_target_pairs={{0,3},{1,2},{2,1},{3,0},{4,7},{5,6},{6,5},{7,4},{8,11},{9,10},{10,... | collective-permute-start | bytes 43016 | tf_op jit(solution)/shard_map/ppermute | solution.py:22

commit v2 on v1

--- a/solution.py
+++ b/solution.py
@@ -8,8 +8,8 @@
 CAP = 4
 EPSILON = 1e-06
 TAIL = 128
-CUTS = 7
-FLIGHT = 4
+CUTS = 4
+AHEAD = 2
 RING = 3
 MIB = 1024 * 1024
 VMEM = pl.BlockSpec(memory_space=pltpu.VMEM)
@@ -97,7 +97,7 @@
     squares = jnp.sum(hidden * hidden, axis=1, keepdims=True) + jnp.sum(other * other, axis=1, keepdims=True)
     row_scale = lax.rsqrt(squares / (2 * half) + EPSILON)
     hidden_ref[...] = hidden
-    packet_ref[:, :half] = (hidden * row_scale * gain_ref[...]).astype(jnp.bfloat16)
+    packet_ref[:, :half] = (hidden * row_scale * gain_ref[...][None, :]).astype(jnp.bfloat16)
     packet_ref[:, half:] = tail_ref[...]
 
 
@@ -184,7 +184,7 @@
 
 def route_kernel(sizes, top, pieces, where_ref, *refs):
     here = refs[:pieces]
-    packed_ref, place_ref, table_ref, rows_ref = refs[pieces:]
+    packed_ref, place_ref, table_ref, count_ref, rows_ref = refs[pieces:]
     each, half = here[0].shape[0], here[0].shape[1] - TAIL
     experts, _, slots = table_ref.shape
     tokens = each * pieces
@@ -215,6 +215,7 @@
         table_ref[e, 0:1, :] = jnp.sum(jnp.where(used, weights[e], 0.0), axis=0, keepdims=True)
         table_ref[e, 1:2, :] = jnp.sum(jnp.where(used, token, 0.0), axis=0, keepdims=True)
         place_ref[e * slots : (e + 1) * slots, :] = jnp.where(used, 1.0, 0.0).T.astype(jnp.bfloat16)
+        count_ref[e] = jnp.sum(jnp.where(lane == e, present, 0.0)).astype(jnp.int32)
     pack(place_ref[...], rows_ref, packed_ref)
 
 
@@ -234,9 +235,10 @@
             jax.ShapeDtypeStruct((experts * slots, half), jnp.bfloat16),
             jax.ShapeDtypeStruct((experts * slots, tokens), jnp.bfloat16),
             jax.ShapeDtypeStruct((experts, 8, slots), jnp.float32),
+            jax.ShapeDtypeStruct((experts,), jnp.int32),
         ),
         in_specs=[SMEM] + [VMEM] * pieces,
-        out_specs=(VMEM, VMEM, VMEM),
+        out_specs=(VMEM, VMEM, VMEM, SMEM),
         scratch_shapes=[pltpu.VMEM((tokens, half), jnp.bfloat16)],
         compiler_params=pltpu.CompilerParams(vmem_limit_bytes=2 * nbytes + 8 * MIB),
         cost_estimate=pl.CostEstimate(
@@ -246,19 +248,18 @@
     )(where, *here)
 
 
-def in_order(copies):
-    for copy in copies[:FLIGHT]:
-        copy.start()
-
-    def wait(index):
-        copies[index].wait()
-        if index + FLIGHT < len(copies):
-            copies[index + FLIGHT].start()
-
-    return wait
-
-
-def hidden_units(where, place, packed, there, gate_held, up_weight):
+def per_count(count, slots, run):
+    last = -1
+    for rows in (slots // 2, slots * 3 // 4, slots):
+
+        @pl.when((count > last) & (count <= rows))
+        def _(rows=rows):
+            run(rows)
+
+        last = rows
+
+
+def hidden_units(where, count, place, packed, there, gate_held, up_weight):
     experts, features, units = up_weight.shape
     half = packed.shape[1]
     slots = packed.shape[0] // experts
@@ -267,20 +268,23 @@
     tokens = place.shape[1]
     each = tokens // pieces
 
-    def kernel(where_ref, place_ref, packed_ref, *refs):
+    def kernel(where_ref, count_ref, place_ref, packed_ref, *refs):
         there_refs, refs = refs[:pieces], refs[pieces:]
         gate_refs, refs = refs[: len(gate_held)], refs[len(gate_held) :]
         up_ref, out_ref, ring_ref, rows_ref, other_ref, ring_sems, sems = refs
-        gate_at = [(ref, e) for ref in gate_refs for e in range(ref.shape[0])]
         mine = pl.ds(pl.multiple_of(where_ref[0] * half, 128), half)
         others = pl.ds(pl.multiple_of((1 - where_ref[0]) * half, 128), half)
-        wait = in_order([
-            pltpu.make_async_copy(
-                up_ref.at[e, rows, :], ring_ref.at[e % depth, rows, :], ring_sems.at[2 * (e % depth) + side]
+
+        def load(e, side):
+            rows = (mine, others)[side]
+            slot = lax.rem(e, depth)
+            return pltpu.make_async_copy(
+                up_ref.at[e, rows, :], ring_ref.at[slot, rows, :], ring_sems.at[2 * slot + side]
             )
-            for e in range(experts)
-            for side, rows in enumerate((mine, others))
-        ])
+
+        for e in range(min(AHEAD, experts)):
+            load(e, 0).start()
+            load(e, 1).start()
         copies = []
         for q in range(pieces):
             span = pl.ds(q * each, each)
@@ -291,24 +295,47 @@
         for copy in copies:
             copy.wait()
         pack(place_ref[...], rows_ref, other_ref)
-        for e in range(experts):
-            span = slice(e * slots, (e + 1) * slots)
-            gate_ref, index = gate_at[e]
-            slot = e % depth
-            gate_act = jnp.dot(packed_ref[span, :], gate_ref[index, mine, :], preferred_element_type=jnp.float32)
-            gate_act += jnp.dot(other_ref[span, :], gate_ref[index, others, :], preferred_element_type=jnp.float32)
-            wait(2 * e)
-            up_act = jnp.dot(packed_ref[span, :], ring_ref[slot, mine, :], preferred_element_type=jnp.float32)
-            wait(2 * e + 1)
-            up_act += jnp.dot(other_ref[span, :], ring_ref[slot, others, :], preferred_element_type=jnp.float32)
-            out_ref[e] = (gate_act / (1.0 + jnp.exp(-gate_act)) * up_act).astype(jnp.bfloat16)
+        def expert(e, gate_ref, index):
+            slot = lax.rem(e, depth)
+            for side in (0, 1):
+                load(e, side).wait()
+
+                @pl.when(e + AHEAD < experts)
+                def _(side=side):
+                    load(e + AHEAD, side).start()
+
+            def run(rows):
+                span = pl.ds(pl.multiple_of(e * slots, slots), rows)
+
+                def project(weight, at):
+                    here = jnp.dot(packed_ref[span, :], weight[at, mine, :], preferred_element_type=jnp.float32)
+                    return here + jnp.dot(other_ref[span, :], weight[at, others, :], preferred_element_type=jnp.float32)
+
+                gate_act = project(gate_ref, index)
+                up_act = project(ring_ref, slot)
+                units_now = gate_act / (1.0 + jnp.exp(-gate_act)) * up_act
+                out_ref[e, 0:rows, :] = units_now.astype(jnp.bfloat16)
+                if rows < slots:
+                    out_ref[e, rows:slots, :] = jnp.zeros((slots - rows, units), jnp.bfloat16)
+
+            per_count(count_ref[e], slots, run)
+
+        done = 0
+        for gate_ref in gate_refs:
+
+            def step(index, carry, done=done, gate_ref=gate_ref):
+                expert(done + index, gate_ref, index)
+                return carry
+
+            lax.fori_loop(0, gate_ref.shape[0], step, 0)
+            done += gate_ref.shape[0]
 
     scratch = depth * features * units * 2 + tokens * half * 2 + experts * slots * half * 2
     work = 4 * experts * slots * half // CUTS + 24 * slots * units + 2 * slots * features
     return pl.pallas_call(
         kernel,
         out_shape=jax.ShapeDtypeStruct((experts, slots, units), jnp.bfloat16),
-        in_specs=[SMEM, VMEM, VMEM] + [ANY] * pieces + [VMEM] * len(gate_held) + [HBM],
+        in_specs=[SMEM, SMEM, VMEM, VMEM] + [ANY] * pieces + [VMEM] * len(gate_held) + [HBM],
         out_specs=VMEM,
         scratch_shapes=[
             pltpu.VMEM((depth, features, units), jnp.bfloat16),
@@ -324,7 +351,7 @@
             transcendentals=experts * slots * units,
         ),
         name="gate_up",
-    )(where, place, packed, *there, *map(in_vmem, gate_held), in_hbm(up_weight))
+    )(where, count, place, packed, *there, *map(in_vmem, gate_held), in_hbm(up_weight))
 
 
 def down(where, table, here, there, down_held, tokens):
@@ -339,17 +366,19 @@
         here_refs, there_refs, refs = refs[:pieces], refs[pieces : 2 * pieces], refs[2 * pieces :]
         down_ref, outs, (units_ref, acc_ref, sems) = refs[0], refs[1:-3], refs[-3:]
         copies = []
-        for q in range(pieces):
-            for side, source in ((0, here_refs[q]), (1, there_refs[q])):
-                owner = (where_ref[0] ^ side) * pieces + (where_ref[2] ^ q)
-                columns = pl.ds(pl.multiple_of(owner * part, 128), part)
-                copies.append(pltpu.make_async_copy(source, units_ref.at[:, :, columns], sems.at[2 * q + side]))
+        for e in range(experts):
+            for q in range(pieces):
+                for side, source in ((0, here_refs[q]), (1, there_refs[q])):
+                    owner = (where_ref[0] ^ side) * pieces + (where_ref[2] ^ q)
+                    columns = pl.ds(pl.multiple_of(owner * part, 128), part)
+                    target = units_ref.at[e, :, columns]
+                    copies.append(pltpu.make_async_copy(source.at[e], target, sems.at[len(copies)]))
         for copy in copies:
             copy.start()
-        for copy in copies:
-            copy.wait()
         token = lax.broadcasted_iota(jnp.int32, (tokens, slots), 0)
         for e in range(experts):
+            for copy in copies[e * 2 * pieces : (e + 1) * 2 * pieces]:
+                copy.wait()
             projected = jnp.dot(units_ref[e], down_ref[e], preferred_element_type=jnp.float32).astype(jnp.bfloat16)
             named = token == table_ref[e, 1:2, :].astype(jnp.int32)
             weights = jnp.where(named, table_ref[e, 0:1, :], 0.0)
@@ -378,9 +407,9 @@
         scratch_shapes=[
             pltpu.VMEM((experts, slots, hidden), jnp.bfloat16),
             pltpu.VMEM((tokens, width), jnp.float32),
-            pltpu.SemaphoreType.DMA((2 * pieces,)),
+            pltpu.SemaphoreType.DMA((experts * 2 * pieces,)),
         ],
-        compiler_params=pltpu.CompilerParams(vmem_limit_bytes=scratch + work + 2 * MIB),
+        compiler_params=pltpu.CompilerParams(vmem_limit_bytes=scratch + work + 4 * MIB),
         cost_estimate=pl.CostEstimate(
             flops=2 * experts * slots * hidden * width,
             bytes_accessed=2 * experts * hidden * width,
@@ -443,24 +472,26 @@
     experts = gate_weight.shape[0]
     attn = attn_part[0]
     there = [swap(attn, "head", 1), swap(residual, "head", 1)]
-    base, tail, gain = prepare(where, attn, residual, routes, gates, norm_gain[None, :])
+    base, tail, gain = prepare(where, attn, residual, routes, gates, norm_gain)
     there, base, tail, gain = lax.optimization_barrier((there, base, tail, gain))
     hidden, packet = norm(where, base, there[0], there[1], gain, tail)
 
     early = experts * 3 // 8
     first = stage([(gate_weight, 0, early)], packet)
     column, first = gather_rows(packet, "req", first)
-    second = stage([(gate_weight, early, experts)], column)
     here = [column] + [swap(column, "grp", bits) for bits in range(1, groups)]
-    here, second = lax.optimization_barrier((here, second))
-    there = [swap(piece, "head", 1) for piece in here]
-    packed, place, table = route(where, here, experts, (reqs, groups, rows), top)
-    units = hidden_units(where, place, packed, there, first + second, up_weight)
+    there = [swap(column, "head", 1)]
+    second = stage([(gate_weight, early, experts)], there[0])
+    here[1:], second = lax.optimization_barrier((here[1:], second))
+    there += [swap(piece, "head", 1) for piece in here[1:]]
+    packed, place, table, count = route(where, here, experts, (reqs, groups, rows), top)
+    units = hidden_units(where, count, place, packed, there, first + second, up_weight)
 
     held = stage([(down_weight, 0, experts)], units)
     here = [units] + [swap(units, "grp", bits) for bits in range(1, groups)]
-    here, held = lax.optimization_barrier((here, held))
-    there = [swap(piece, "head", 1) for piece in here]
+    there = [swap(units, "head", 1)]
+    here[1:], held = lax.optimization_barrier((here[1:], held))
+    there += [swap(piece, "head", 1) for piece in here[1:]]
     partial = down(where, table, here, there, held[0], tokens)
 
     if reqs > 4:

time: 92.8 us -> 92.5 us (level)
  waiting for transfers between devices: 16.2 us -> 18.2 us
  local copies, waits for them, and re-layouts: 1.33 us -> 0 us
    pallas_call x1, Pallas kernels: 7.38 us -> 9.85 us  [down(): pl.pallas_call(kernel, out_shape=shapes, in_specs=[SMEM, VMEM] + [ANY] *...]
    pallas_call x1, Pallas kernels: 16.4 us -> 14.2 us  [hidden_units(): pl.pallas_call(kernel, out_shape=jax.ShapeDtypeStruct((experts, slots, un...]
    ppermute x25, waiting for transfers between devices: 16.2 us -> 18.2 us  [swap(): lax.ppermute(array, axis, [(i, i ^ bits) for i in range(lax.axis_size(axi...]
    broadcast_in_dim x1 -> x0, local copies, waits for them, and re-layouts: 1.33 us -> none  [on_device(): norm_gain[None, :]]
    ppermute x25, starting transfers between devices: 23.3 us -> 22.4 us  [swap(): lax.ppermute(array, axis, [(i, i ^ bits) for i in range(lax.axis_size(axi...]
  transfers between devices with their start and end apart: 25 -> 25, of which waited for: 13 -> 13; matrix products, arithmetic and copies ran while one was open for 2% -> 0% of each run, Pallas kernels for 27% -> 27%
where the time goes in v2:
time: 92.5 us; the launch traced here: 92.3 us
  Pallas kernels  51.4 us (56%)
  starting transfers between devices  22.4 us (24%)
  waiting for transfers between devices  18.2 us (20%)
    ppermute x25, starting transfers between devices, swap(): lax.ppermute(array, axis, [(i, i ^ bits) for i in range(lax.axis_size(axi...  22.4 us
    pallas_call x3, Pallas kernels, stage(): pl.pallas_call(kernel, out_shape=[pltpu.VMEM((end - first, *array.shape[1...  20 us
    ppermute x25, waiting for transfers between devices, swap(): lax.ppermute(array, axis, [(i, i ^ bits) for i in range(lax.axis_size(axi...  18.2 us
    pallas_call x1, Pallas kernels, hidden_units(): pl.pallas_call(kernel, out_shape=jax.ShapeDtypeStruct((experts, slots, un...  14.2 us
    pallas_call x1, Pallas kernels, down(): pl.pallas_call(kernel, out_shape=shapes, in_specs=[SMEM, VMEM] + [ANY] *...  9.85 us
    pallas_call x1, Pallas kernels, route(): pl.pallas_call(kernel, out_shape=(jax.ShapeDtypeStruct((experts * slots,...  3.31 us
  transfers between devices with their start and end apart: 25, of which 13 were waited for; matrix products, arithmetic and copies ran while one was open for 0% of the time, Pallas kernels for 27%

profile of v2, /device:TPU:0, one launch (start us, length us, event | category | flops | bytes accessed | tf_op | source)
XLA Modules:
  0.0 92.3 jit_solution(11091602160692506149)
XLA Ops:
  0.0 0.5 collective-permute-start
  0.5 0.1 collective-permute-start.1
  0.5 0.1 pad_add_fusion.where_ref.refs_0_
  0.6 1.6 %prepare.1 = (f32[8,7168]{1,0:T(8,128)S(1)}, bf16[8,128]{1,0:T(8,128)(2,1)S(1)}, f32[3584]{0:T(1024)S(1)}) custom-call(s32[3]{0:T(128)S(1)} %pad_add_fusion.where_ref.refs_0_, bf16[8,7168]{1,0:T(8,128)(2,1)} %bitcast.13, bf16[8,3584]{1,0:T(8,128)(2,1)} %refs_1_.1, s32[8,8]{1,0:T(8,128)} %refs_2_.1, f32[8,8]{1,0:T(8,128)} %refs_3_.1, f32[3584]{0:T(1024)} %refs_4_.1), custom_call_target="tpu_custom_call" | custom-call | tf_op jit(solution)/shard_map/prepare/pallas_call | solution.py:75
  2.2 0.0 collective-permute-done.1.res_there_ref
  2.2 0.7 norm.1
  2.9 3.1 %collective-permute-start.2 = (bf16[8,3712]{1,0:T(8,128)(2,1)S(1)}, bf16[8,3712]{1,0:T(8,128)(2,1)S(1)}, u32[]{:S(2)}, u32[]{:S(2)}) collective-permute-start(bf16[8,3712]{1,0:T(8,128)(2,1)S(1)} %get-tuple-element.50.refs_1_.refs_0_), channel_id=1, source_target_pairs={{0,8},{8,0},{16,24},{24,16},{1,9},{9,1},{17,25},{25,17},{2,10},{10... | collective-permute-start | bytes 178184 | tf_op jit(solution)/shard_map/ppermute | solution.py:22
  6.0 2.6 %collective-permute-start.3 = (bf16[8,3712]{1,0:T(8,128)(2,1)S(1)}, bf16[8,3712]{1,0:T(8,128)(2,1)S(1)}, u32[]{:S(2)}, u32[]{:S(2)}) collective-permute-start(bf16[8,3712]{1,0:T(8,128)(2,1)S(1)} %get-tuple-element.50.refs_1_.refs_0_), channel_id=1, source_target_pairs={{0,16},{8,24},{16,0},{24,8},{1,17},{9,25},{17,1},{25,9},{2,18},{10... | collective-permute-start | bytes 178184 | tf_op jit(solution)/shard_map/ppermute | solution.py:22
  8.6 0.0 collective-permute-start.4
  8.6 4.2 %stage.3.refs_4_ = bf16[3,7168,256]{2,1,0:T(8,128)(2,1)S(1)} custom-call(bf16[8,7168,256]{2,1,0:T(8,128)(2,1)} %refs_0_.4, bf16[8,3712]{1,0:T(8,128)(2,1)S(1)} %get-tuple-element.50.refs_1_.refs_0_), custom_call_target="tpu_custom_call" | custom-call | bytes 11010048 | tf_op jit(solution)/shard_map/stage/pallas_call | solution.py:147
  12.8 0.0 collective-permute-done.2.refs_1_
  12.8 1.7 %collective-permute-done.4.refs_3_ = bf16[8,3712]{1,0:T(8,128)(2,1)S(1)} collective-permute-done((bf16[8,3712]{1,0:T(8,128)(2,1)S(1)}, bf16[8,3712]{1,0:T(8,128)(2,1)S(1)}, u32[]{:S(2)}, u32[]{:S(2)}) %collective-permute-start.4) | collective-permute-done | bytes 59424 | tf_op jit(solution)/shard_map/ppermute | solution.py:22
  14.6 0.1 collective-permute-start.8
  14.7 1.6 %collective-permute-start.5 = (bf16[32,3712]{1,0:T(8,128)(2,1)S(1)}, bf16[32,3712]{1,0:T(8,128)(2,1)S(1)}, u32[]{:S(2)}, u32[]{:S(2)}) collective-permute-start(bf16[32,3712]{1,0:T(8,128)(2,1)S(1)} %collect.1.refs_1_), channel_id=1, source_target_pairs={{0,1},{1,0},{2,3},{3,2},{4,5},{5,4},{6,7},{7,6},{8,9},{9,8},{10,11... | collective-permute-start | bytes 712712 | tf_op jit(solution)/shard_map/ppermute | solution.py:22
  16.3 1.5 %collective-permute-start.6 = (bf16[32,3712]{1,0:T(8,128)(2,1)S(1)}, bf16[32,3712]{1,0:T(8,128)(2,1)S(1)}, u32[]{:S(2)}, u32[]{:S(2)}) collective-permute-start(bf16[32,3712]{1,0:T(8,128)(2,1)S(1)} %collect.1.refs_1_), channel_id=1, source_target_pairs={{0,2},{1,3},{2,0},{3,1},{4,6},{5,7},{6,4},{7,5},{8,10},{9,11},{10,... | collective-permute-start | bytes 712712 | tf_op jit(solution)/shard_map/ppermute | solution.py:22
  17.8 0.5 collective-permute-start.7
  18.3 6.3 %stage.4.refs_5_ = bf16[5,7168,256]{2,1,0:T(8,128)(2,1)S(1)} custom-call(bf16[8,7168,256]{2,1,0:T(8,128)(2,1)} %refs_0_.4, bf16[32,3712]{1,0:T(8,128)(2,1)S(1)} %collective-permute-done.8.refs_1_.refs_0_), custom_call_target="tpu_custom_call" | custom-call | bytes 18350080 | tf_op jit(solution)/shard_map/stage/pallas_call | solution.py:147
  24.6 4.6 %collective-permute-done.6.refs_3_ = bf16[32,3712]{1,0:T(8,128)(2,1)S(1)} collective-permute-done((bf16[32,3712]{1,0:T(8,128)(2,1)S(1)}, bf16[32,3712]{1,0:T(8,128)(2,1)S(1)}, u32[]{:S(2)}, u32[]{:S(2)}) %collective-permute-start.6) | collective-permute-done | bytes 237600 | tf_op jit(solution)/shard_map/ppermute | solution.py:22
  29.2 0.5 collective-permute-start.10
  29.7 0.0 collective-permute-start.11
  29.7 3.3 %route.1 = (bf16[512,3584]{1,0:T(8,128)(2,1)S(1)}, bf16[512,128]{1,0:T(8,128)(2,1)S(1)}, f32[8,8,64]{2,1,0:T(8,128)S(1)}, s32[8]{0:T(128)S(1)}) custom-call(s32[3]{0:T(128)S(1)} %pad_add_fusion.where_ref.refs_0_, bf16[32,3712]{1,0:T(8,128)(2,1)S(1)} %collect.1.refs_1_, bf16[32,3712]{1,0:T(8,128)(2,1)S(1)} %collective-permute-done.5.refs_2_, ...), custom_call_target="tpu_custom_call" | custom-call | flops 469762048 | bytes 7340032 | tf_op jit(solution)/shard_map/route/pallas_call | solution.py:232
  33.1 14.2 %gate_up.1.refs_1_.refs_0_ = bf16[8,64,256]{2,1,0:T(8,128)(2,1)S(1)} custom-call(s32[3]{0:T(128)S(1)} %pad_add_fusion.where_ref.refs_0_, s32[8]{0:T(128)S(1)} %get-tuple-element.58.count_ref, bf16[512,128]{1,0:T(8,128)(2,1)S(1)} %get-tuple-element.59.place_ref, bf16[512,3584]{1,0:T(8,128)(2,1)S(1)} %get-tuple-element.60.packed_ref, ...), custom_call_target="tpu_custom_call" | custom-call | flops 3758096384 | bytes 29360128 | tf_op jit(solution)/shard_map/gate_up/pallas_call | solution.py:335
  47.2 1.3 %collective-permute-start.12 = (bf16[8,64,256]{2,1,0:T(8,128)(2,1)S(1)}, bf16[8,64,256]{2,1,0:T(8,128)(2,1)S(1)}, u32[]{:S(2)}, u32[]{:S(2)}) collective-permute-start(bf16[8,64,256]{2,1,0:T(8,128)(2,1)S(1)} %gate_up.1.refs_1_.refs_0_), channel_id=1, source_target_pairs={{0,1},{1,0},{2,3},{3,2},{4,5},{5,4},{6,7},{7,6},{8,9},{9,8},{10,11... | collective-permute-start | bytes 786440 | tf_op jit(solution)/shard_map/ppermute | solution.py:22
  48.5 0.8 collective-permute-start.13
  49.4 1.4 %collective-permute-start.14 = (bf16[8,64,256]{2,1,0:T(8,128)(2,1)S(1)}, bf16[8,64,256]{2,1,0:T(8,128)(2,1)S(1)}, u32[]{:S(2)}, u32[]{:S(2)}) collective-permute-start(bf16[8,64,256]{2,1,0:T(8,128)(2,1)S(1)} %gate_up.1.refs_1_.refs_0_), channel_id=1, source_target_pairs={{0,3},{1,2},{2,1},{3,0},{4,7},{5,6},{6,5},{7,4},{8,11},{9,10},{10,... | collective-permute-start | bytes 786440 | tf_op jit(solution)/shard_map/ppermute | solution.py:22
  50.8 9.5 %stage.5.refs_8_ = bf16[8,2048,896]{2,1,0:T(8,128)(2,1)S(1)} custom-call(bf16[8,2048,896]{2,1,0:T(8,128)(2,1)} %refs_0_.5, bf16[8,64,256]{2,1,0:T(8,128)(2,1)S(1)} %gate_up.1.refs_1_.refs_0_), custom_call_target="tpu_custom_call" | custom-call | bytes 29360128 | tf_op jit(solution)/shard_map/stage/pallas_call | solution.py:147
  60.3 0.7 collective-permute-done.13.refs_2_
  61.0 1.6 %collective-permute-done.14.refs_3_ = bf16[8,64,256]{2,1,0:T(8,128)(2,1)S(1)} collective-permute-done((bf16[8,64,256]{2,1,0:T(8,128)(2,1)S(1)}, bf16[8,64,256]{2,1,0:T(8,128)(2,1)S(1)}, u32[]{:S(2)}, u32[]{:S(2)}) %collective-permute-start.14) | collective-permute-done | bytes 262176 | tf_op jit(solution)/shard_map/ppermute | solution.py:22
  62.6 0.5 collective-permute-start.17
  63.1 0.0 collective-permute-start.18
  63.1 1.0 %collective-permute-done.16.refs_5_ = bf16[8,64,256]{2,1,0:T(8,128)(2,1)S(1)} collective-permute-done((bf16[8,64,256]{2,1,0:T(8,128)(2,1)S(1)}, bf16[8,64,256]{2,1,0:T(8,128)(2,1)S(1)}, u32[]{:S(2)}, u32[]{:S(2)}) %collective-permute-start.16) | collective-permute-done | bytes 262176 | tf_op jit(solution)/shard_map/ppermute | solution.py:22
  64.1 0.4 collective-permute-done.17.refs_6_
  64.5 0.4 collective-permute-done.18.refs_7_
  64.9 9.8 %down.1 = (bf16[32,896]{1,0:T(8,128)(2,1)S(1)}, bf16[32,896]{1,0:T(8,128)(2,1)S(1)}, bf16[32,896]{1,0:T(8,128)(2,1)S(1)}, bf16[32,896]{1,0:T(8,128)(2,1)S(1)}) custom-call(s32[3]{0:T(128)S(1)} %pad_add_fusion.where_ref.refs_0_, f32[8,8,64]{2,1,0:T(8,128)S(1)} %get-tuple-element.57.table_ref, bf16[8,64,256]{2,1,0:T(8,128)(2,1)S(1)} %gate_up.1.refs_1_.refs_0_, ...), custom_call_target="tpu_custom_call" | custom-call | flops 1879048192 | bytes 29360128 | tf_op jit(solution)/shard_map/down/pallas_call | solution.py:402
  74.7 0.1 collective-permute-start.19
  74.8 2.6 %collective-permute-start.20 = (bf16[32,896]{1,0:T(8,128)(2,1)S(1)}, bf16[32,896]{1,0:T(8,128)(2,1)S(1)}, u32[]{:S(2)}, u32[]{:S(2)}) collective-permute-start(bf16[32,896]{1,0:T(8,128)(2,1)S(1)} %get-tuple-element.69), channel_id=1, source_target_pairs={{0,16},{8,24},{16,0},{24,8},{1,17},{9,25},{17,1},{25,9},{2,18},{10... | collective-permute-start | bytes 172040 | tf_op jit(solution)/shard_map/ppermute | solution.py:22
  77.4 1.8 %collective-permute-start.21 = (bf16[32,896]{1,0:T(8,128)(2,1)S(1)}, bf16[32,896]{1,0:T(8,128)(2,1)S(1)}, u32[]{:S(2)}, u32[]{:S(2)}) collective-permute-start(bf16[32,896]{1,0:T(8,128)(2,1)S(1)} %get-tuple-element.70), channel_id=1, source_target_pairs={{0,24},{8,16},{16,8},{24,0},{1,25},{9,17},{17,9},{25,1},{2,26},{10... | collective-permute-start | bytes 172040 | tf_op jit(solution)/shard_map/ppermute | solution.py:22
  79.2 0.7 collective-permute-done.19
  79.9 2.2 %collective-permute-done.20 = bf16[32,896]{1,0:T(8,128)(2,1)S(1)} collective-permute-done((bf16[32,896]{1,0:T(8,128)(2,1)S(1)}, bf16[32,896]{1,0:T(8,128)(2,1)S(1)}, u32[]{:S(2)}, u32[]{:S(2)}) %collective-permute-start.20) | collective-permute-done | bytes 57376 | tf_op jit(solution)/shard_map/ppermute | solution.py:22
  82.1 1.4 %collective-permute-done.21 = bf16[32,896]{1,0:T(8,128)(2,1)S(1)} collective-permute-done((bf16[32,896]{1,0:T(8,128)(2,1)S(1)}, bf16[32,896]{1,0:T(8,128)(2,1)S(1)}, u32[]{:S(2)}, u32[]{:S(2)}) %collective-permute-start.21) | collective-permute-done | bytes 57376 | tf_op jit(solution)/shard_map/ppermute | solution.py:22
  83.5 0.6 sum_req.1
  84.1 0.8 collective-permute-start.22
  84.9 1.5 %collective-permute-start.23 = (bf16[8,896]{1,0:T(8,128)(2,1)S(1)}, bf16[8,896]{1,0:T(8,128)(2,1)S(1)}, u32[]{:S(2)}, u32[]{:S(2)}) collective-permute-start(bf16[8,896]{1,0:T(8,128)(2,1)S(1)} %get-tuple-element.73), channel_id=1, source_target_pairs={{0,2},{1,3},{2,0},{3,1},{4,6},{5,7},{6,4},{7,5},{8,10},{9,11},{10,... | collective-permute-start | bytes 43016 | tf_op jit(solution)/shard_map/ppermute | solution.py:22
  86.5 1.2 %collective-permute-start.24 = (bf16[8,896]{1,0:T(8,128)(2,1)S(1)}, bf16[8,896]{1,0:T(8,128)(2,1)S(1)}, u32[]{:S(2)}, u32[]{:S(2)}) collective-permute-start(bf16[8,896]{1,0:T(8,128)(2,1)S(1)} %get-tuple-element.74), channel_id=1, source_target_pairs={{0,3},{1,2},{2,1},{3,0},{4,7},{5,6},{6,5},{7,4},{8,11},{9,10},{10,... | collective-permute-start | bytes 43016 | tf_op jit(solution)/shard_map/ppermute | solution.py:22
  87.7 0.2 collective-permute-done.22.refs_1_
  87.9 0.8 collective-permute-done.23.refs_2_
  88.7 2.4 %collective-permute-done.24.refs_3_ = bf16[8,896]{1,0:T(8,128)(2,1)S(1)} collective-permute-done((bf16[8,896]{1,0:T(8,128)(2,1)S(1)}, bf16[8,896]{1,0:T(8,128)(2,1)S(1)}, u32[]{:S(2)}, u32[]{:S(2)}) %collective-permute-start.24) | collective-permute-done | bytes 14368 | tf_op jit(solution)/shard_map/ppermute | solution.py:22
  91.1 1.2 %mix.1 = bf16[8,3584]{1,0:T(8,128)(2,1)} custom-call(s32[3]{0:T(128)S(1)} %pad_add_fusion.where_ref.refs_0_, f32[8,3584]{1,0:T(8,128)S(1)} %get-tuple-element.48.hidden_ref, bf16[8,896]{1,0:T(8,128)(2,1)S(1)} %get-tuple-element.71.refs_0_, bf16[8,896]{1,0:T(8,128)(2,1)S(1)} %collective-permute-done.22.refs_1_, ...), custom_call_target="tpu_custom_call" | custom-call | tf_op jit(solution)/shard_map/mix/pallas_call | solution.py:456
  (14 shorter events, 0.1 us)
Async XLA Ops:
  0.0 2.2 %collective-permute-start = (bf16[8,7168]{1,0:T(8,128)(2,1)}, bf16[8,7168]{1,0:T(8,128)(2,1)S(1)}, u32[]{:S(2)}, u32[]{:S(2)}) collective-permute-start(bf16[8,7168]{1,0:T(8,128)(2,1)} %bitcast.12), channel_id=1, source_target_pairs={{0,4},{4,0},{1,5},{5,1},{2,6},{6,2},{3,7},{7,3},{8,12},{12,8},{9,1... | collective-permute-start | bytes 344072 | tf_op jit(solution)/shard_map/ppermute | solution.py:22
  0.5 1.7 %collective-permute-start.1 = (bf16[8,3584]{1,0:T(8,128)(2,1)}, bf16[8,3584]{1,0:T(8,128)(2,1)S(1)}, u32[]{:S(2)}, u32[]{:S(2)}) collective-permute-start(bf16[8,3584]{1,0:T(8,128)(2,1)} %refs_1_.1), channel_id=1, source_target_pairs={{0,4},{4,0},{1,5},{5,1},{2,6},{6,2},{3,7},{7,3},{8,12},{12,8},{9,1... | collective-permute-start | bytes 172040 | tf_op jit(solution)/shard_map/ppermute | solution.py:22
  2.9 9.9 %collective-permute-start.2 = (bf16[8,3712]{1,0:T(8,128)(2,1)S(1)}, bf16[8,3712]{1,0:T(8,128)(2,1)S(1)}, u32[]{:S(2)}, u32[]{:S(2)}) collective-permute-start(bf16[8,3712]{1,0:T(8,128)(2,1)S(1)} %get-tuple-element.50.refs_1_.refs_0_), channel_id=1, source_target_pairs={{0,8},{8,0},{16,24},{24,16},{1,9},{9,1},{17,25},{25,17},{2,10},{10... | collective-permute-start | bytes 178184 | tf_op jit(solution)/shard_map/ppermute | solution.py:22
  6.0 6.8 %collective-permute-start.3 = (bf16[8,3712]{1,0:T(8,128)(2,1)S(1)}, bf16[8,3712]{1,0:T(8,128)(2,1)S(1)}, u32[]{:S(2)}, u32[]{:S(2)}) collective-permute-start(bf16[8,3712]{1,0:T(8,128)(2,1)S(1)} %get-tuple-element.50.refs_1_.refs_0_), channel_id=1, source_target_pairs={{0,16},{8,24},{16,0},{24,8},{1,17},{9,25},{17,1},{25,9},{2,18},{10... | collective-permute-start | bytes 178184 | tf_op jit(solution)/shard_map/ppermute | solution.py:22
  8.6 6.0 %collective-permute-start.4 = (bf16[8,3712]{1,0:T(8,128)(2,1)S(1)}, bf16[8,3712]{1,0:T(8,128)(2,1)S(1)}, u32[]{:S(2)}, u32[]{:S(2)}) collective-permute-start(bf16[8,3712]{1,0:T(8,128)(2,1)S(1)} %get-tuple-element.50.refs_1_.refs_0_), channel_id=1, source_target_pairs={{0,24},{8,16},{16,8},{24,0},{1,25},{9,17},{17,9},{25,1},{2,26},{10... | collective-permute-start | bytes 178184 | tf_op jit(solution)/shard_map/ppermute | solution.py:22
  14.6 3.6 %collective-permute-start.8 = (bf16[32,3712]{1,0:T(8,128)(2,1)S(1)}, bf16[32,3712]{1,0:T(8,128)(2,1)S(1)}, u32[]{:S(2)}, u32[]{:S(2)}) collective-permute-start(bf16[32,3712]{1,0:T(8,128)(2,1)S(1)} %collect.1.refs_1_), channel_id=1, source_target_pairs={{0,4},{4,0},{1,5},{5,1},{2,6},{6,2},{3,7},{7,3},{8,12},{12,8},{9,1... | collective-permute-start | bytes 712712 | tf_op jit(solution)/shard_map/ppermute | solution.py:22
  14.7 9.9 %collective-permute-start.5 = (bf16[32,3712]{1,0:T(8,128)(2,1)S(1)}, bf16[32,3712]{1,0:T(8,128)(2,1)S(1)}, u32[]{:S(2)}, u32[]{:S(2)}) collective-permute-start(bf16[32,3712]{1,0:T(8,128)(2,1)S(1)} %collect.1.refs_1_), channel_id=1, source_target_pairs={{0,1},{1,0},{2,3},{3,2},{4,5},{5,4},{6,7},{7,6},{8,9},{9,8},{10,11... | collective-permute-start | bytes 712712 | tf_op jit(solution)/shard_map/ppermute | solution.py:22
  16.3 12.9 %collective-permute-start.6 = (bf16[32,3712]{1,0:T(8,128)(2,1)S(1)}, bf16[32,3712]{1,0:T(8,128)(2,1)S(1)}, u32[]{:S(2)}, u32[]{:S(2)}) collective-permute-start(bf16[32,3712]{1,0:T(8,128)(2,1)S(1)} %collect.1.refs_1_), channel_id=1, source_target_pairs={{0,2},{1,3},{2,0},{3,1},{4,6},{5,7},{6,4},{7,5},{8,10},{9,11},{10,... | collective-permute-start | bytes 712712 | tf_op jit(solution)/shard_map/ppermute | solution.py:22
  17.8 11.4 %collective-permute-start.7 = (bf16[32,3712]{1,0:T(8,128)(2,1)S(1)}, bf16[32,3712]{1,0:T(8,128)(2,1)S(1)}, u32[]{:S(2)}, u32[]{:S(2)}) collective-permute-start(bf16[32,3712]{1,0:T(8,128)(2,1)S(1)} %collect.1.refs_1_), channel_id=1, source_target_pairs={{0,3},{1,2},{2,1},{3,0},{4,7},{5,6},{6,5},{7,4},{8,11},{9,10},{10,... | collective-permute-start | bytes 712712 | tf_op jit(solution)/shard_map/ppermute | solution.py:22
  29.2 3.8 %collective-permute-start.9 = (bf16[32,3712]{1,0:T(8,128)(2,1)S(1)}, bf16[32,3712]{1,0:T(8,128)(2,1)S(1)}, u32[]{:S(2)}, u32[]{:S(2)}) collective-permute-start(bf16[32,3712]{1,0:T(8,128)(2,1)S(1)} %collective-permute-done.5.refs_2_), channel_id=1, source_target_pairs={{0,4},{4,0},{1,5},{5,1},{2,6},{6,2},{3,7},{7,3},{8,12},{12,8},{9,1... | collective-permute-start | bytes 712712 | tf_op jit(solution)/shard_map/ppermute | solution.py:22
  29.2 3.8 %collective-permute-start.10 = (bf16[32,3712]{1,0:T(8,128)(2,1)S(1)}, bf16[32,3712]{1,0:T(8,128)(2,1)S(1)}, u32[]{:S(2)}, u32[]{:S(2)}) collective-permute-start(bf16[32,3712]{1,0:T(8,128)(2,1)S(1)} %collective-permute-done.6.refs_3_), channel_id=1, source_target_pairs={{0,4},{4,0},{1,5},{5,1},{2,6},{6,2},{3,7},{7,3},{8,12},{12,8},{9,1... | collective-permute-start | bytes 712712 | tf_op jit(solution)/shard_map/ppermute | solution.py:22
  29.7 3.3 %collective-permute-start.11 = (bf16[32,3712]{1,0:T(8,128)(2,1)S(1)}, bf16[32,3712]{1,0:T(8,128)(2,1)S(1)}, u32[]{:S(2)}, u32[]{:S(2)}) collective-permute-start(bf16[32,3712]{1,0:T(8,128)(2,1)S(1)} %collective-permute-done.7.refs_4_), channel_id=1, source_target_pairs={{0,4},{4,0},{1,5},{5,1},{2,6},{6,2},{3,7},{7,3},{8,12},{12,8},{9,1... | collective-permute-start | bytes 712712 | tf_op jit(solution)/shard_map/ppermute | solution.py:22
  47.2 13.1 %collective-permute-start.12 = (bf16[8,64,256]{2,1,0:T(8,128)(2,1)S(1)}, bf16[8,64,256]{2,1,0:T(8,128)(2,1)S(1)}, u32[]{:S(2)}, u32[]{:S(2)}) collective-permute-start(bf16[8,64,256]{2,1,0:T(8,128)(2,1)S(1)} %gate_up.1.refs_1_.refs_0_), channel_id=1, source_target_pairs={{0,1},{1,0},{2,3},{3,2},{4,5},{5,4},{6,7},{7,6},{8,9},{9,8},{10,11... | collective-permute-start | bytes 786440 | tf_op jit(solution)/shard_map/ppermute | solution.py:22
  48.5 12.4 %collective-permute-start.13 = (bf16[8,64,256]{2,1,0:T(8,128)(2,1)S(1)}, bf16[8,64,256]{2,1,0:T(8,128)(2,1)S(1)}, u32[]{:S(2)}, u32[]{:S(2)}) collective-permute-start(bf16[8,64,256]{2,1,0:T(8,128)(2,1)S(1)} %gate_up.1.refs_1_.refs_0_), channel_id=1, source_target_pairs={{0,2},{1,3},{2,0},{3,1},{4,6},{5,7},{6,4},{7,5},{8,10},{9,11},{10,... | collective-permute-start | bytes 786440 | tf_op jit(solution)/shard_map/ppermute | solution.py:22
  49.4 13.2 %collective-permute-start.14 = (bf16[8,64,256]{2,1,0:T(8,128)(2,1)S(1)}, bf16[8,64,256]{2,1,0:T(8,128)(2,1)S(1)}, u32[]{:S(2)}, u32[]{:S(2)}) collective-permute-start(bf16[8,64,256]{2,1,0:T(8,128)(2,1)S(1)} %gate_up.1.refs_1_.refs_0_), channel_id=1, source_target_pairs={{0,3},{1,2},{2,1},{3,0},{4,7},{5,6},{6,5},{7,4},{8,11},{9,10},{10,... | collective-permute-start | bytes 786440 | tf_op jit(solution)/shard_map/ppermute | solution.py:22
  50.8 12.3 %collective-permute-start.15 = (bf16[8,64,256]{2,1,0:T(8,128)(2,1)S(1)}, bf16[8,64,256]{2,1,0:T(8,128)(2,1)S(1)}, u32[]{:S(2)}, u32[]{:S(2)}) collective-permute-start(bf16[8,64,256]{2,1,0:T(8,128)(2,1)S(1)} %gate_up.1.refs_1_.refs_0_), channel_id=1, source_target_pairs={{0,4},{4,0},{1,5},{5,1},{2,6},{6,2},{3,7},{7,3},{8,12},{12,8},{9,1... | collective-permute-start | bytes 786440 | tf_op jit(solution)/shard_map/ppermute | solution.py:22
  62.6 1.5 %collective-permute-start.16 = (bf16[8,64,256]{2,1,0:T(8,128)(2,1)S(1)}, bf16[8,64,256]{2,1,0:T(8,128)(2,1)S(1)}, u32[]{:S(2)}, u32[]{:S(2)}) collective-permute-start(bf16[8,64,256]{2,1,0:T(8,128)(2,1)S(1)} %collective-permute-done.12.refs_1_), channel_id=1, source_target_pairs={{0,4},{4,0},{1,5},{5,1},{2,6},{6,2},{3,7},{7,3},{8,12},{12,8},{9,1... | collective-permute-start | bytes 786440 | tf_op jit(solution)/shard_map/ppermute | solution.py:22
  62.6 1.9 %collective-permute-start.17 = (bf16[8,64,256]{2,1,0:T(8,128)(2,1)S(1)}, bf16[8,64,256]{2,1,0:T(8,128)(2,1)S(1)}, u32[]{:S(2)}, u32[]{:S(2)}) collective-permute-start(bf16[8,64,256]{2,1,0:T(8,128)(2,1)S(1)} %collective-permute-done.13.refs_2_), channel_id=1, source_target_pairs={{0,4},{4,0},{1,5},{5,1},{2,6},{6,2},{3,7},{7,3},{8,12},{12,8},{9,1... | collective-permute-start | bytes 786440 | tf_op jit(solution)/shard_map/ppermute | solution.py:22
  63.1 1.8 %collective-permute-start.18 = (bf16[8,64,256]{2,1,0:T(8,128)(2,1)S(1)}, bf16[8,64,256]{2,1,0:T(8,128)(2,1)S(1)}, u32[]{:S(2)}, u32[]{:S(2)}) collective-permute-start(bf16[8,64,256]{2,1,0:T(8,128)(2,1)S(1)} %collective-permute-done.14.refs_3_), channel_id=1, source_target_pairs={{0,4},{4,0},{1,5},{5,1},{2,6},{6,2},{3,7},{7,3},{8,12},{12,8},{9,1... | collective-permute-start | bytes 786440 | tf_op jit(solution)/shard_map/ppermute | solution.py:22
  74.7 5.2 %collective-permute-start.19 = (bf16[32,896]{1,0:T(8,128)(2,1)S(1)}, bf16[32,896]{1,0:T(8,128)(2,1)S(1)}, u32[]{:S(2)}, u32[]{:S(2)}) collective-permute-start(bf16[32,896]{1,0:T(8,128)(2,1)S(1)} %get-tuple-element.68), channel_id=1, source_target_pairs={{0,8},{8,0},{16,24},{24,16},{1,9},{9,1},{17,25},{25,17},{2,10},{10... | collective-permute-start | bytes 172040 | tf_op jit(solution)/shard_map/ppermute | solution.py:22
  74.8 7.3 %collective-permute-start.20 = (bf16[32,896]{1,0:T(8,128)(2,1)S(1)}, bf16[32,896]{1,0:T(8,128)(2,1)S(1)}, u32[]{:S(2)}, u32[]{:S(2)}) collective-permute-start(bf16[32,896]{1,0:T(8,128)(2,1)S(1)} %get-tuple-element.69), channel_id=1, source_target_pairs={{0,16},{8,24},{16,0},{24,8},{1,17},{9,25},{17,1},{25,9},{2,18},{10... | collective-permute-start | bytes 172040 | tf_op jit(solution)/shard_map/ppermute | solution.py:22
  77.4 6.1 %collective-permute-start.21 = (bf16[32,896]{1,0:T(8,128)(2,1)S(1)}, bf16[32,896]{1,0:T(8,128)(2,1)S(1)}, u32[]{:S(2)}, u32[]{:S(2)}) collective-permute-start(bf16[32,896]{1,0:T(8,128)(2,1)S(1)} %get-tuple-element.70), channel_id=1, source_target_pairs={{0,24},{8,16},{16,8},{24,0},{1,25},{9,17},{17,9},{25,1},{2,26},{10... | collective-permute-start | bytes 172040 | tf_op jit(solution)/shard_map/ppermute | solution.py:22
  84.1 3.8 %collective-permute-start.22 = (bf16[8,896]{1,0:T(8,128)(2,1)S(1)}, bf16[8,896]{1,0:T(8,128)(2,1)S(1)}, u32[]{:S(2)}, u32[]{:S(2)}) collective-permute-start(bf16[8,896]{1,0:T(8,128)(2,1)S(1)} %get-tuple-element.72), channel_id=1, source_target_pairs={{0,1},{1,0},{2,3},{3,2},{4,5},{5,4},{6,7},{7,6},{8,9},{9,8},{10,11... | collective-permute-start | bytes 43016 | tf_op jit(solution)/shard_map/ppermute | solution.py:22
  84.9 3.7 %collective-permute-start.23 = (bf16[8,896]{1,0:T(8,128)(2,1)S(1)}, bf16[8,896]{1,0:T(8,128)(2,1)S(1)}, u32[]{:S(2)}, u32[]{:S(2)}) collective-permute-start(bf16[8,896]{1,0:T(8,128)(2,1)S(1)} %get-tuple-element.73), channel_id=1, source_target_pairs={{0,2},{1,3},{2,0},{3,1},{4,6},{5,7},{6,4},{7,5},{8,10},{9,11},{10,... | collective-permute-start | bytes 43016 | tf_op jit(solution)/shard_map/ppermute | solution.py:22
  86.5 4.6 %collective-permute-start.24 = (bf16[8,896]{1,0:T(8,128)(2,1)S(1)}, bf16[8,896]{1,0:T(8,128)(2,1)S(1)}, u32[]{:S(2)}, u32[]{:S(2)}) collective-permute-start(bf16[8,896]{1,0:T(8,128)(2,1)S(1)} %get-tuple-element.74), channel_id=1, source_target_pairs={{0,3},{1,2},{2,1},{3,0},{4,7},{5,6},{6,5},{7,4},{8,11},{9,10},{10,... | collective-permute-start | bytes 43016 | tf_op jit(solution)/shard_map/ppermute | solution.py:22
